TPU v7x, 32 devices: a whole 2x2x4 slice. The times are simulated.
32 devices in a mesh: groups: 2 (over y), row: 4 (over z), col: 4 (over x, core).
Axes of the slice: x: 2, y: 2, z: 4, core: 2. Of those that a mesh axis runs over, the one named last changes fastest.
Arguments:
- queries: bfloat16 [8, 512, 512], P(('groups', 'col'), 'row'), parts along dimension 0, may hold values from -6 to 6
- keys: bfloat16 [8, 512, 128], P(('groups', 'row'), 'col'), parts along dimension 0, may hold values from -6 to 6
- values: bfloat16 [8, 512, 128], P(('groups', 'row'), 'col'), parts along dimension 0, may hold values from -6 to 6
- block_list: int32 [8, 4, 4, 4], P('groups'), parts along dimension 0, may hold values from 0 to 3, as said below
- block_count: int32 [8, 4, 4], P('groups'), parts along dimension 0, may hold values from 0 to 4, as said below
Outputs:
- attended: bfloat16 [8, 512, 512], P(('groups', 'col'), 'row'), parts along dimension 0
There are 2 independent parts, one for each index of `groups`. A program takes and returns all parts, laid end to end along the dimension named above; each array names one. Nothing has to cross between parts.
Inputs may be any that keep to these rules, and one draw needn't show every extreme that they name: For query block i = c * 4 + q, the first block_count[c, q, r] entries of block_list[c, q, r] are distinct positions j in increasing order of key blocks r * 4 + j that do not lie after block i; block i itself is always listed in its panel; the remaining entries are other positions of the panel and carry no meaning. `block_count`: some query block lists all 4 blocks of some panel in every draw.
All inputs are finite; a program needn't handle non-finite values.
Results may differ from a plain program's by a relative error of at most 0.0036.
Values may be sent and summed in bfloat16 or wider, within the bound.
No kernel may reach another device: no remote copies, remote signals or barrier semaphores. Data moves between devices by JAX's collectives and lax.ppermute only.
A program may use at most 64 MiB of HBM per device.

v0:
```python
import functools
import math

import jax
import jax.numpy as jnp
from jax import lax
from jax.experimental import pallas as pl
from jax.experimental.pallas import tpu as pltpu
from jax.sharding import PartitionSpec as P

BLOCK = 128
CORES = 2

floor_score = -1e30
floor_top = -1e20


def join_kernel(transpose, *refs):
    out_ref = refs[-1]
    first = 0
    for ref in refs[:-1]:
        if not transpose:
            out_ref[first : first + ref.shape[0]] = ref[...]
        for n in range(ref.shape[0] if transpose else 0):
            out_ref[first + n, :BLOCK, :] = ref[n, :BLOCK, :]
            out_ref[first + n, BLOCK:, :] = ref[n, BLOCK:, :].T
        first += ref.shape[0]


def prepare_kernel(per, places, dense, list_hbm, count_hbm, order_ref, active_ref, list_ref, count_ref, sems):
    own_blocks = order_ref.shape[0]
    panels, slots = list_ref.shape[1:]
    cols = lax.axis_size("col")
    col_index = lax.axis_index("col")
    row_index = lax.axis_index("row")
    first = row_index * own_blocks
    copies = (
        pltpu.make_async_copy(list_hbm.at[col_index, pl.ds(first, own_blocks)], list_ref, sems.at[0]),
        pltpu.make_async_copy(count_hbm.at[col_index, pl.ds(first, own_blocks)], count_ref, sems.at[1]),
    )
    for copy in copies:
        copy.start()
    for copy in copies:
        copy.wait()
    for s in range(own_blocks):
        diagonal = col_index * list_hbm.shape[1] + first + s
        for r in range(panels):
            for n in range(slots):
                active_ref[r * slots + n] = 0
            for n in reversed(range(slots)):
                active_ref[r * slots + list_ref[s, r, n]] = (n < count_ref[s, r]).astype(jnp.int32)
        for part, where in enumerate(places):
            total = jnp.int32(0)
            diagonal_slot = jnp.int32(-1)
            for n, (row_flip, col_flip) in enumerate(where):
                for k in range(per):
                    slot = n * per + k
                    block = ((row_index ^ row_flip) * cols + (col_index ^ col_flip)) * per + k
                    on_diagonal = block == diagonal
                    if dense:
                        reach = jnp.where(on_diagonal, 0, jnp.where(active_ref[block] > 0, BLOCK, -BLOCK))
                        order_ref[s, part, slot : slot + 1, :] = jnp.full((1, order_ref.shape[3]), reach, jnp.int32)
                        continue
                    order_ref[s, part, total] = slot
                    diagonal_slot = jnp.where(on_diagonal, slot, diagonal_slot)
                    total = total + jnp.where(on_diagonal, 0, active_ref[block])
            if dense:
                continue
            end = order_ref.shape[2] - 2
            here = diagonal_slot >= 0
            order_ref[s, part, total] = diagonal_slot
            order_ref[s, part, end + 1] = jnp.where(here, total, -1)
            total = total + here.astype(jnp.int32)
            order_ref[s, part, total] = 0
            order_ref[s, part, end] = total


def blockwise(array, fold):
    return fold(array.reshape(array.shape[0] // 8, 8, array.shape[1]), axis=0)


def dense_attention(reach, kv_ref, queries, score_ref):
    head_size, width = queries.shape
    slots = kv_ref.shape[0]
    factor = math.log2(math.e) / head_size**0.5
    key_at = lax.broadcasted_iota(jnp.int32, (BLOCK, width), 0)
    query_at = lax.broadcasted_iota(jnp.int32, (BLOCK, width), 1) % BLOCK
    keys = jnp.concatenate([kv_ref[slot, :BLOCK, :] for slot in range(slots)])
    found = jnp.dot(keys, queries, preferred_element_type=jnp.float32)
    top = jnp.full((8, width), floor_top, jnp.float32)
    for slot in range(slots):
        seen = query_at + reach[slot : slot + 1, :] >= key_at
        one = jnp.where(seen, found[slot * BLOCK : (slot + 1) * BLOCK], floor_score)
        score_ref[slot] = one
        top = jnp.maximum(top, blockwise(one, jnp.max))
    top = jnp.max(top, axis=0, keepdims=True) * factor
    denom = jnp.zeros((8, width), jnp.float32)
    rounded = []
    for slot in range(slots):
        one = jnp.exp2(score_ref[slot] * factor - top)
        denom = denom + blockwise(one, jnp.sum)
        rounded.append(one.astype(jnp.bfloat16))
    values = jnp.concatenate([kv_ref[slot, BLOCK:, :] for slot in range(slots)], axis=1)
    acc = jnp.dot(values, jnp.concatenate(rounded), preferred_element_type=jnp.float32)
    return acc, top, jnp.sum(denom, axis=0, keepdims=True)


def listed_attention(s, part, order_ref, kv_ref, queries, score_ref, acc_ref):
    head_size, width = queries.shape
    end = order_ref.shape[2] - 2
    factor = math.log2(math.e) / head_size**0.5
    total = order_ref[s, part, end]
    diagonal = order_ref[s, part, end + 1]
    pairs = (total + 1) // 2
    key_at = lax.broadcasted_iota(jnp.int32, (BLOCK, width), 0)
    query_at = lax.broadcasted_iota(jnp.int32, (BLOCK, width), 1) % BLOCK

    def score(p, top):
        pair = [order_ref[s, part, 2 * p + n] for n in range(2)]
        keys = jnp.concatenate([kv_ref[slot, :BLOCK, :] for slot in pair])
        found = jnp.dot(keys, queries, preferred_element_type=jnp.float32)
        for n in range(2):
            t = 2 * p + n
            reach = jnp.where(t == diagonal, 0, jnp.where(t < total, BLOCK, -BLOCK))
            one = jnp.where(query_at + reach >= key_at, found[n * BLOCK : (n + 1) * BLOCK], floor_score)
            score_ref[t] = one
            top = jnp.maximum(top, blockwise(one, jnp.max))
        return top

    top = lax.fori_loop(0, pairs, score, jnp.full((8, width), floor_top, jnp.float32))
    top = jnp.max(top, axis=0, keepdims=True) * factor
    acc_ref[...] = jnp.zeros_like(acc_ref)

    def mix(p, denom):
        pair = [order_ref[s, part, 2 * p + n] for n in range(2)]
        values = jnp.concatenate([kv_ref[slot, BLOCK:, :] for slot in pair], axis=1)
        weights = [jnp.exp2(score_ref[2 * p + n] * factor - top) for n in range(2)]
        rounded = jnp.concatenate([one.astype(jnp.bfloat16) for one in weights])
        acc_ref[...] += jnp.dot(values, rounded, preferred_element_type=jnp.float32)
        return denom + blockwise(weights[0] + weights[1], jnp.sum)

    denom = lax.fori_loop(0, pairs, mix, jnp.zeros((8, width), jnp.float32))
    return acc_ref[...], top, jnp.sum(denom, axis=0, keepdims=True)


def get_order(dense, order_ref, scratch):
    if dense:
        return order_ref
    held, sem = scratch
    copy = pltpu.make_async_copy(order_ref, held, sem)
    copy.start()
    copy.wait()
    return held


def attention(dense, s, part, order_ref, kv_ref, queries, score_ref, acc_ref):
    if dense:
        return dense_attention(order_ref[s, part], kv_ref, queries, score_ref)
    return listed_attention(s, part, order_ref, kv_ref, queries, score_ref, acc_ref)


def turn_kernel(heads, q_ref, qt_ref):
    own_blocks, head_size = qt_ref.shape[:2]
    for s in range(own_blocks):
        for h in range(heads):
            tile = q_ref[0, pl.ds(s * BLOCK, BLOCK), pl.ds(h * head_size, head_size)]
            qt_ref[s, :, pl.ds(h * BLOCK, BLOCK)] = tile.T


def early_kernel(heads, dense, qt_ref, order_in, kv_ref, acc_out, stats_out, score_ref, acc_ref, *scratch):
    order_ref = get_order(dense, order_in, scratch)
    for s in range(qt_ref.shape[0]):
        acc, top, denom = attention(dense, s, 0, order_ref, kv_ref, qt_ref[s], score_ref, acc_ref)
        acc_out[s] = acc
        stats_out[s, 0:1] = top
        stats_out[s, 1:2] = denom


def last_kernel(per, places, heads, dense, qt_ref, order_in, kv_ref, acc_in, stats_in, out_hbm,
                out_ref, out_sems, score_ref, acc_ref, *scratch):
    order_ref = get_order(dense, order_in, scratch)
    own_blocks, head_size, width = qt_ref.shape
    rows, cols = lax.axis_size("row"), lax.axis_size("col")
    row_index, col_index = lax.axis_index("row"), lax.axis_index("col")
    sources = [(row_index ^ row_flip) * cols + (col_index ^ col_flip) for row_flip, col_flip in places]
    earliest = functools.reduce(jnp.minimum, sources) * per

    for s in range(own_blocks):
        useful = earliest <= (col_index * rows + row_index) * own_blocks + s

        def finish(acc, scale):
            copies = []
            for h in range(heads):
                at = pl.ds(h * head_size, head_size)
                cut = slice(h * BLOCK, (h + 1) * BLOCK)
                one = acc_in[s, :, cut] * scale[:, cut]
                if acc is not None:
                    one = one + acc[:, cut]
                out_ref[0, pl.ds(s * BLOCK, BLOCK), at] = one.astype(out_ref.dtype).T
                place = (0, pl.ds(s * BLOCK, BLOCK), at)
                copies.append(pltpu.make_async_copy(out_ref.at[place], out_hbm.at[place], out_sems.at[s, h]))
                copies[-1].start()
            for copy in copies:
                copy.wait()

        @pl.when(useful)
        def _():
            acc, top, denom = attention(dense, s, 1, order_ref, kv_ref, qt_ref[s], score_ref, acc_ref)
            other_top, other_denom = stats_in[s, 0:1], stats_in[s, 1:2]
            overall = jnp.maximum(top, other_top)
            scale, other_scale = jnp.exp2(top - overall), jnp.exp2(other_top - overall)
            share = 1.0 / (scale * denom + other_scale * other_denom)
            finish(acc * (scale * share), other_scale * share)

        @pl.when(jnp.logical_not(useful))
        def _():
            finish(None, 1.0 / stats_in[s, 1:2])


def swap(piece, axis, flip):
    array, places = piece
    came = lax.ppermute(array, axis, [(i, i ^ flip) for i in range(lax.axis_size(axis))])
    if axis == "row":
        return came, [(r ^ flip, c) for r, c in places]
    return came, [(r, c ^ flip) for r, c in places]


def join_pieces(pieces, transpose=True):
    vmem = pl.BlockSpec(memory_space=pltpu.VMEM)
    first = pieces[0][0]
    blocks = sum(array.shape[0] for array, _ in pieces)
    array = pl.pallas_call(
        functools.partial(join_kernel, transpose),
        out_shape=jax.ShapeDtypeStruct((blocks,) + first.shape[1:], first.dtype),
        in_specs=[vmem] * len(pieces),
        out_specs=vmem,
        compiler_params=pltpu.CompilerParams(vmem_limit_bytes=4 * 1024 * 1024),
        name="join",
    )(*(array for array, _ in pieces))
    return array, [place for _, places in pieces for place in places]


def together(pieces, *others):
    arrays = lax.optimization_barrier([array for array, _ in pieces] + list(others))
    held = [(array, places) for array, (_, places) in zip(arrays, pieces)]
    return (held, *arrays[len(held) :]) if others else held


def across(piece, cols):
    pieces = [piece]
    flip = CORES
    while flip < cols:
        pieces += [swap(one, "col", flip) for one in pieces]
        flip *= 2
    return pieces[1:]


def per_device(queries, keys, values, block_list, block_count):
    head_size = keys.shape[2]
    heads = queries.shape[2] // head_size
    own_blocks = queries.shape[1] // BLOCK
    per = keys.shape[1] // BLOCK
    rows = lax.axis_size("row")
    cols = lax.axis_size("col")
    panels, slots = block_list.shape[2:]
    blocks = panels * slots
    vmem = pl.BlockSpec(memory_space=pltpu.VMEM)
    smem = pl.BlockSpec(memory_space=pltpu.SMEM)
    anywhere = pl.BlockSpec(memory_space=pl.ANY)
    small = pltpu.CompilerParams(vmem_limit_bytes=4 * 1024 * 1024)

    shape = (per, BLOCK, head_size)
    packed = jnp.concatenate([keys.reshape(shape), values.reshape(shape)], axis=1)

    own = (packed, [(0, 0)])
    flip = rows // 2
    while flip > 2:
        came = swap(own, "row", flip)
        own = jnp.concatenate([own[0], came[0]]), own[1] + came[1]
        flip //= 2
    near, far, opposite = (swap(own, "row", flip) for flip in (1, 2, 3))
    own_across = across(own, cols)
    near_across = [swap(piece, "row", 1) for piece in own_across]
    early_places = [place for _, where in (own, *own_across, near, *near_across, far, opposite) for place in where]
    late_places = [(r, c ^ flip) for flip in range(CORES, cols, CORES) for r, c in far[1] + opposite[1]]
    places = [where + [(r, c ^ 1) for r, c in where] for where in (early_places, late_places)]

    longest = max(len(where) for where in places) * per
    dense = longest <= 16
    width = heads * BLOCK
    order_shape = (own_blocks, len(places), longest, width) if dense else (own_blocks, len(places), longest + 3)
    order = pl.pallas_call(
        functools.partial(prepare_kernel, per, places, dense),
        out_shape=jax.ShapeDtypeStruct(order_shape, jnp.int32),
        in_specs=[anywhere, anywhere],
        out_specs=vmem if dense else smem,
        scratch_shapes=[
            pltpu.SMEM((blocks,), jnp.int32),
            pltpu.SMEM((own_blocks, panels, slots), jnp.int32),
            pltpu.SMEM((own_blocks, panels), jnp.int32),
            pltpu.SemaphoreType.DMA((2,)),
        ],
        compiler_params=small,
        name="prepare",
    )(block_list, block_count)
    (far,), order = together([far], order)
    last = across(far, cols) + across(opposite, cols)
    halves = [join_pieces([own, *own_across]), join_pieces([near, *near_across]), join_pieces([far, opposite])]
    early = join_pieces(halves + [swap(half, "col", 1) for half in halves], False)

    def attend(kernel, name, out_shape, out_specs, scratch, *args):
        held = args[2].shape[0] + args[2].shape[0] % 2
        scratch = scratch + [
            pltpu.VMEM((held, BLOCK, width), jnp.float32),
            pltpu.VMEM((head_size, width), jnp.float32),
        ]
        if not dense:
            scratch += [pltpu.SMEM(order.shape, jnp.int32), pltpu.SemaphoreType.DMA]
        return pl.pallas_call(
            functools.partial(kernel, heads, dense),
            out_shape=out_shape,
            in_specs=[vmem, vmem if dense else anywhere] + [vmem] * (len(args) - 2),
            out_specs=out_specs,
            scratch_shapes=scratch,
            compiler_params=pltpu.CompilerParams(vmem_limit_bytes=2 * held * BLOCK * width * 4 + 8 * 1024 * 1024),
            name=name,
        )(*args)

    queries_across = pl.pallas_call(
        functools.partial(turn_kernel, heads),
        out_shape=jax.ShapeDtypeStruct((own_blocks, head_size, width), queries.dtype),
        in_specs=[vmem],
        out_specs=vmem,
        compiler_params=small,
        name="turn",
    )(queries)
    last, queries_across = together(last, queries_across)
    parts = (
        jax.ShapeDtypeStruct((own_blocks, head_size, width), jnp.float32),
        jax.ShapeDtypeStruct((own_blocks, 2, width), jnp.float32),
    )
    part = attend(early_kernel, "early", parts, (vmem, vmem), [], queries_across, order, early[0])
    last = join_pieces(last)
    last_pair, *part = together([swap(last, "col", 1)], *part)
    last = join_pieces([last, *last_pair], False)
    whole = jax.ShapeDtypeStruct(queries.shape, jnp.bfloat16)
    out_scratch = [pltpu.VMEM(queries.shape, jnp.bfloat16), pltpu.SemaphoreType.DMA((own_blocks, heads))]
    end = functools.partial(last_kernel, per, places[1])
    return attend(end, "last", whole, anywhere, out_scratch, queries_across, order, last[0], *part)


def solution(mesh):
    placed = (
        P(("groups", "col"), "row", None),
        P(("groups", "row"), "col", None),
        P(("groups", "row"), "col", None),
        P("groups", None, None, None),
        P("groups", None, None),
    )
    return jax.shard_map(
        per_device,
        mesh=mesh,
        in_specs=placed,
        out_specs=P(("groups", "col"), "row", None),
        check_vma=False,
    )
```

profile of v0, /device:TPU:21, one launch (start us, length us, event | category | flops | bytes accessed | tf_op | source)
XLA Modules:
  0.0 20.6 jit_solution(5994723366682022141)
XLA Ops:
  0.0 0.8 %constant_dynamic-update-slice_fusion.1 = bf16[1,256,128]{2,1,0:T(8,128)(2,1)S(1)} fusion(bf16[1,128,128]{2,1,0:T(8,128)(2,1)} %param.6), kind=kLoop, calls=%fused_computation.1 | loop fusion | bytes 65536
  0.8 0.8 %constant_dynamic-update-slice_fusion.refs_0_ = bf16[1,256,128]{2,1,0:T(8,128)(2,1)S(1)} fusion(bf16[1,256,128]{2,1,0:T(8,128)(2,1)S(1)} %constant_dynamic-update-slice_fusion.1, bf16[1,128,128]{2,1,0:T(8,128)(2,1)} %param.7), kind=kLoop, calls=%fused_computation | loop fusion | bytes 65536 | tf_op jit(solution)/shard_map/concatenate | solution.py:273
  1.6 0.1 collective-permute-start
  1.6 1.2 %collective-permute-start.5 = (bf16[1,256,128]{2,1,0:T(8,128)(2,1)S(1)}, bf16[1,256,128]{2,1,0:T(8,128)(2,1)S(1)}, u32[]{:S(2)}, u32[]{:S(2)}) collective-permute-start(bf16[1,256,128]{2,1,0:T(8,128)(2,1)S(1)} %constant_dynamic-update-slice_fusion.refs_0_), channel_id=1, source_target_pairs={{0,2},{1,3},{2,0},{3,1},{4,6},{5,7},{6,4},{7,5},{8,10},{9,11},{10,... | collective-permute-start | bytes 196616 | tf_op jit(solution)/shard_map/ppermute | solution.py:222
  2.8 2.4 %collective-permute-start.2 = (bf16[1,256,128]{2,1,0:T(8,128)(2,1)S(1)}, bf16[1,256,128]{2,1,0:T(8,128)(2,1)S(1)}, u32[]{:S(2)}, u32[]{:S(2)}) collective-permute-start(bf16[1,256,128]{2,1,0:T(8,128)(2,1)S(1)} %constant_dynamic-update-slice_fusion.refs_0_), channel_id=1, source_target_pairs={{0,12},{4,8},{8,4},{12,0},{1,13},{5,9},{9,5},{13,1},{2,14},{6,10},... | collective-permute-start | bytes 196616 | tf_op jit(solution)/shard_map/ppermute | solution.py:222
  5.3 1.1 %collective-permute-start.6 = (bf16[1,256,128]{2,1,0:T(8,128)(2,1)S(1)}, bf16[1,256,128]{2,1,0:T(8,128)(2,1)S(1)}, u32[]{:S(2)}, u32[]{:S(2)}) collective-permute-start(bf16[1,256,128]{2,1,0:T(8,128)(2,1)S(1)} %constant_dynamic-update-slice_fusion.refs_0_), channel_id=1, source_target_pairs={{0,4},{4,0},{8,12},{12,8},{1,5},{5,1},{9,13},{13,9},{2,6},{6,2},{1... | collective-permute-start | bytes 196616 | tf_op jit(solution)/shard_map/ppermute | solution.py:222
  6.3 0.8 %copy-done.1 = s32[4,4,4,4]{3,2,1,0:T(4,128)S(1)} copy-done((s32[4,4,4,4]{3,2,1,0:T(4,128)S(1)}, s32[4,4,4,4]{3,2,1,0:T(4,128)}, u32[]{:S(2)}) %copy-start.1) | copy-done | bytes 1048
  7.1 0.7 %copy-done.2 = s32[4,4,4]{2,1,0:T(4,128)S(1)} copy-done((s32[4,4,4]{2,1,0:T(4,128)S(1)}, s32[4,4,4]{2,1,0:T(4,128)}, u32[]{:S(2)}) %copy-start.2) | copy-done | bytes 280
  7.8 0.7 %prepare.1.order_in = s32[1,2,12,512]{3,2,1,0:T(8,128)S(1)} custom-call(s32[4,4,4,4]{3,2,1,0:T(4,128)S(1)} %copy-done.1, s32[4,4,4]{2,1,0:T(4,128)S(1)} %copy-done.2), custom_call_target="tpu_custom_call" | custom-call | tf_op jit(solution)/shard_map/prepare/pallas_call | solution.py:292
  8.4 0.0 collective-permute-done.refs_0_
  8.5 0.0 collective-permute-done.5.refs_1_
  8.5 0.5 %collective-permute-start.7 = (bf16[1,256,128]{2,1,0:T(8,128)(2,1)S(1)}, bf16[1,256,128]{2,1,0:T(8,128)(2,1)S(1)}, u32[]{:S(2)}, u32[]{:S(2)}) collective-permute-start(bf16[1,256,128]{2,1,0:T(8,128)(2,1)S(1)} %collective-permute-done.5.refs_1_), channel_id=1, source_target_pairs={{0,4},{4,0},{8,12},{12,8},{1,5},{5,1},{9,13},{13,9},{2,6},{6,2},{1... | collective-permute-start | bytes 196616 | tf_op jit(solution)/shard_map/ppermute | solution.py:222
  8.9 1.7 %collective-permute-start.1 = (bf16[1,256,128]{2,1,0:T(8,128)(2,1)S(1)}, bf16[1,256,128]{2,1,0:T(8,128)(2,1)S(1)}, u32[]{:S(2)}, u32[]{:S(2)}) collective-permute-start(bf16[1,256,128]{2,1,0:T(8,128)(2,1)S(1)} %collective-permute-done.refs_0_), channel_id=1, source_target_pairs={{0,2},{1,3},{2,0},{3,1},{4,6},{5,7},{6,4},{7,5},{8,10},{9,11},{10,... | collective-permute-start | bytes 196616 | tf_op jit(solution)/shard_map/ppermute | solution.py:222
  10.6 0.0 collective-permute-done.2.refs_1_
  10.6 0.9 %collective-permute-start.3 = (bf16[1,256,128]{2,1,0:T(8,128)(2,1)S(1)}, bf16[1,256,128]{2,1,0:T(8,128)(2,1)S(1)}, u32[]{:S(2)}, u32[]{:S(2)}) collective-permute-start(bf16[1,256,128]{2,1,0:T(8,128)(2,1)S(1)} %collective-permute-done.2.refs_1_), channel_id=1, source_target_pairs={{0,2},{1,3},{2,0},{3,1},{4,6},{5,7},{6,4},{7,5},{8,10},{9,11},{10,... | collective-permute-start | bytes 196616 | tf_op jit(solution)/shard_map/ppermute | solution.py:222
  11.6 0.1 turn.1.qt_ref
  11.6 0.1 join.9.refs_2_
  11.7 1.7 %collective-permute-start.10 = (bf16[2,256,128]{2,1,0:T(8,128)(2,1)S(1)}, bf16[2,256,128]{2,1,0:T(8,128)(2,1)S(1)}, u32[]{:S(2)}, u32[]{:S(2)}) collective-permute-start(bf16[2,256,128]{2,1,0:T(8,128)(2,1)S(1)} %join.9.refs_2_), channel_id=1, source_target_pairs={{0,1},{1,0},{2,3},{3,2},{4,5},{5,4},{6,7},{7,6},{8,9},{9,8},{10,11... | collective-permute-start | bytes 393224 | tf_op jit(solution)/shard_map/ppermute | solution.py:222
  13.5 0.1 join.7.refs_0_
  13.5 0.0 collective-permute-done.6.refs_0_
  13.5 0.1 collective-permute-start.8
  13.6 0.0 collective-permute-done.7.refs_1_
  13.6 0.1 join.8.refs_1_
  13.7 1.0 %collective-permute-start.9 = (bf16[2,256,128]{2,1,0:T(8,128)(2,1)S(1)}, bf16[2,256,128]{2,1,0:T(8,128)(2,1)S(1)}, u32[]{:S(2)}, u32[]{:S(2)}) collective-permute-start(bf16[2,256,128]{2,1,0:T(8,128)(2,1)S(1)} %join.8.refs_1_), channel_id=1, source_target_pairs={{0,1},{1,0},{2,3},{3,2},{4,5},{5,4},{6,7},{7,6},{8,9},{9,8},{10,11... | collective-permute-start | bytes 393224 | tf_op jit(solution)/shard_map/ppermute | solution.py:222
  14.7 0.0 collective-permute-done.3.refs_1_
  14.7 0.1 join.6.refs_0_
  14.8 2.8 %collective-permute-start.4 = (bf16[2,256,128]{2,1,0:T(8,128)(2,1)S(1)}, bf16[2,256,128]{2,1,0:T(8,128)(2,1)S(1)}, u32[]{:S(2)}, u32[]{:S(2)}) collective-permute-start(bf16[2,256,128]{2,1,0:T(8,128)(2,1)S(1)} %join.6.refs_0_), channel_id=1, source_target_pairs={{0,1},{1,0},{2,3},{3,2},{4,5},{5,4},{6,7},{7,6},{8,9},{9,8},{10,11... | collective-permute-start | bytes 393224 | tf_op jit(solution)/shard_map/ppermute | solution.py:222
  17.6 0.0 collective-permute-done.10.refs_5_
  17.6 0.1 join.10.kv_ref
  17.7 1.5 %early.1 = (f32[1,128,512]{2,1,0:T(8,128)S(1)}, f32[1,2,512]{2,1,0:T(2,128)S(1)}) custom-call(bf16[1,128,512]{2,1,0:T(8,128)(2,1)S(1)} %turn.1.qt_ref, s32[1,2,12,512]{3,2,1,0:T(8,128)S(1)} %prepare.1.order_in, bf16[12,256,128]{2,1,0:T(8,128)(2,1)S(1)} %join.10.kv_ref), custom_call_target="tpu_custom_call" | custom-call | tf_op jit(solution)/shard_map/early/pallas_call | solution.py:319
  19.2 0.0 collective-permute-done.4.refs_1_
  19.2 1.4 %last.1 = bf16[1,128,512]{2,1,0:T(8,128)(2,1)} custom-call(bf16[1,128,512]{2,1,0:T(8,128)(2,1)S(1)} %turn.1.qt_ref, s32[1,2,12,512]{3,2,1,0:T(8,128)S(1)} %prepare.1.order_in, bf16[4,256,128]{2,1,0:T(8,128)(2,1)S(1)} %join.11.kv_ref, f32[1,128,512]{2,1,0:T(8,128)S(1)} %get-tuple-element.23.acc_in, f32[1,2,512]{2,1,0:T(2,128)S(1)} %get-tuple-element.24.stats_in), custom_call_target="tpu_custom_call" | custom-call | tf_op jit(solution)/shard_map/last/pallas_call | solution.py:319
  (8 shorter events, 0.0 us)
Async XLA Ops:
  0.0 11.6 %copy-start = (bf16[1,128,512]{2,1,0:T(8,128)(2,1)S(1)}, bf16[1,128,512]{2,1,0:T(8,128)(2,1)}, u32[]{:S(2)}) copy-start(bf16[1,128,512]{2,1,0:T(8,128)(2,1)} %q_ref.1) | copy-start | bytes 393220
  1.6 6.9 %collective-permute-start = (bf16[1,256,128]{2,1,0:T(8,128)(2,1)S(1)}, bf16[1,256,128]{2,1,0:T(8,128)(2,1)S(1)}, u32[]{:S(2)}, u32[]{:S(2)}) collective-permute-start(bf16[1,256,128]{2,1,0:T(8,128)(2,1)S(1)} %constant_dynamic-update-slice_fusion.refs_0_), channel_id=1, source_target_pairs={{0,8},{4,12},{8,0},{12,4},{1,9},{5,13},{9,1},{13,5},{2,10},{6,14},... | collective-permute-start | bytes 196616 | tf_op jit(solution)/shard_map/ppermute | solution.py:222
  1.6 6.8 %collective-permute-start.5 = (bf16[1,256,128]{2,1,0:T(8,128)(2,1)S(1)}, bf16[1,256,128]{2,1,0:T(8,128)(2,1)S(1)}, u32[]{:S(2)}, u32[]{:S(2)}) collective-permute-start(bf16[1,256,128]{2,1,0:T(8,128)(2,1)S(1)} %constant_dynamic-update-slice_fusion.refs_0_), channel_id=1, source_target_pairs={{0,2},{1,3},{2,0},{3,1},{4,6},{5,7},{6,4},{7,5},{8,10},{9,11},{10,... | collective-permute-start | bytes 196616 | tf_op jit(solution)/shard_map/ppermute | solution.py:222
  2.8 7.8 %collective-permute-start.2 = (bf16[1,256,128]{2,1,0:T(8,128)(2,1)S(1)}, bf16[1,256,128]{2,1,0:T(8,128)(2,1)S(1)}, u32[]{:S(2)}, u32[]{:S(2)}) collective-permute-start(bf16[1,256,128]{2,1,0:T(8,128)(2,1)S(1)} %constant_dynamic-update-slice_fusion.refs_0_), channel_id=1, source_target_pairs={{0,12},{4,8},{8,4},{12,0},{1,13},{5,9},{9,5},{13,1},{2,14},{6,10},... | collective-permute-start | bytes 196616 | tf_op jit(solution)/shard_map/ppermute | solution.py:222
  5.3 8.3 %collective-permute-start.6 = (bf16[1,256,128]{2,1,0:T(8,128)(2,1)S(1)}, bf16[1,256,128]{2,1,0:T(8,128)(2,1)S(1)}, u32[]{:S(2)}, u32[]{:S(2)}) collective-permute-start(bf16[1,256,128]{2,1,0:T(8,128)(2,1)S(1)} %constant_dynamic-update-slice_fusion.refs_0_), channel_id=1, source_target_pairs={{0,4},{4,0},{8,12},{12,8},{1,5},{5,1},{9,13},{13,9},{2,6},{6,2},{1... | collective-permute-start | bytes 196616 | tf_op jit(solution)/shard_map/ppermute | solution.py:222
  6.3 0.8 %copy-start.1 = (s32[4,4,4,4]{3,2,1,0:T(4,128)S(1)}, s32[4,4,4,4]{3,2,1,0:T(4,128)}, u32[]{:S(2)}) copy-start(s32[4,4,4,4]{3,2,1,0:T(4,128)} %list_hbm.1) | copy-start | bytes 3076
  7.1 0.7 %copy-start.2 = (s32[4,4,4]{2,1,0:T(4,128)S(1)}, s32[4,4,4]{2,1,0:T(4,128)}, u32[]{:S(2)}) copy-start(s32[4,4,4]{2,1,0:T(4,128)} %count_hbm.1) | copy-start | bytes 772
  8.5 5.2 %collective-permute-start.7 = (bf16[1,256,128]{2,1,0:T(8,128)(2,1)S(1)}, bf16[1,256,128]{2,1,0:T(8,128)(2,1)S(1)}, u32[]{:S(2)}, u32[]{:S(2)}) collective-permute-start(bf16[1,256,128]{2,1,0:T(8,128)(2,1)S(1)} %collective-permute-done.5.refs_1_), channel_id=1, source_target_pairs={{0,4},{4,0},{8,12},{12,8},{1,5},{5,1},{9,13},{13,9},{2,6},{6,2},{1... | collective-permute-start | bytes 196616 | tf_op jit(solution)/shard_map/ppermute | solution.py:222
  8.9 5.8 %collective-permute-start.1 = (bf16[1,256,128]{2,1,0:T(8,128)(2,1)S(1)}, bf16[1,256,128]{2,1,0:T(8,128)(2,1)S(1)}, u32[]{:S(2)}, u32[]{:S(2)}) collective-permute-start(bf16[1,256,128]{2,1,0:T(8,128)(2,1)S(1)} %collective-permute-done.refs_0_), channel_id=1, source_target_pairs={{0,2},{1,3},{2,0},{3,1},{4,6},{5,7},{6,4},{7,5},{8,10},{9,11},{10,... | collective-permute-start | bytes 196616 | tf_op jit(solution)/shard_map/ppermute | solution.py:222
  10.6 4.1 %collective-permute-start.3 = (bf16[1,256,128]{2,1,0:T(8,128)(2,1)S(1)}, bf16[1,256,128]{2,1,0:T(8,128)(2,1)S(1)}, u32[]{:S(2)}, u32[]{:S(2)}) collective-permute-start(bf16[1,256,128]{2,1,0:T(8,128)(2,1)S(1)} %collective-permute-done.2.refs_1_), channel_id=1, source_target_pairs={{0,2},{1,3},{2,0},{3,1},{4,6},{5,7},{6,4},{7,5},{8,10},{9,11},{10,... | collective-permute-start | bytes 196616 | tf_op jit(solution)/shard_map/ppermute | solution.py:222
  11.7 5.9 %collective-permute-start.10 = (bf16[2,256,128]{2,1,0:T(8,128)(2,1)S(1)}, bf16[2,256,128]{2,1,0:T(8,128)(2,1)S(1)}, u32[]{:S(2)}, u32[]{:S(2)}) collective-permute-start(bf16[2,256,128]{2,1,0:T(8,128)(2,1)S(1)} %join.9.refs_2_), channel_id=1, source_target_pairs={{0,1},{1,0},{2,3},{3,2},{4,5},{5,4},{6,7},{7,6},{8,9},{9,8},{10,11... | collective-permute-start | bytes 393224 | tf_op jit(solution)/shard_map/ppermute | solution.py:222
  13.5 4.1 %collective-permute-start.8 = (bf16[2,256,128]{2,1,0:T(8,128)(2,1)S(1)}, bf16[2,256,128]{2,1,0:T(8,128)(2,1)S(1)}, u32[]{:S(2)}, u32[]{:S(2)}) collective-permute-start(bf16[2,256,128]{2,1,0:T(8,128)(2,1)S(1)} %join.7.refs_0_), channel_id=1, source_target_pairs={{0,1},{1,0},{2,3},{3,2},{4,5},{5,4},{6,7},{7,6},{8,9},{9,8},{10,11... | collective-permute-start | bytes 393224 | tf_op jit(solution)/shard_map/ppermute | solution.py:222
  13.7 3.9 %collective-permute-start.9 = (bf16[2,256,128]{2,1,0:T(8,128)(2,1)S(1)}, bf16[2,256,128]{2,1,0:T(8,128)(2,1)S(1)}, u32[]{:S(2)}, u32[]{:S(2)}) collective-permute-start(bf16[2,256,128]{2,1,0:T(8,128)(2,1)S(1)} %join.8.refs_1_), channel_id=1, source_target_pairs={{0,1},{1,0},{2,3},{3,2},{4,5},{5,4},{6,7},{7,6},{8,9},{9,8},{10,11... | collective-permute-start | bytes 393224 | tf_op jit(solution)/shard_map/ppermute | solution.py:222
  14.8 4.3 %collective-permute-start.4 = (bf16[2,256,128]{2,1,0:T(8,128)(2,1)S(1)}, bf16[2,256,128]{2,1,0:T(8,128)(2,1)S(1)}, u32[]{:S(2)}, u32[]{:S(2)}) collective-permute-start(bf16[2,256,128]{2,1,0:T(8,128)(2,1)S(1)} %join.6.refs_0_), channel_id=1, source_target_pairs={{0,1},{1,0},{2,3},{3,2},{4,5},{5,4},{6,7},{7,6},{8,9},{9,8},{10,11... | collective-permute-start | bytes 393224 | tf_op jit(solution)/shard_map/ppermute | solution.py:222
where the time goes:
time: 20.9 us; the launch traced here: 20.6 us
  starting transfers between devices  13.4 us (64%)
  Pallas kernels  4.01 us (19%)
  local copies, waits for them, and re-layouts  3.02 us (14%)
    ppermute x11, starting transfers between devices, swap(): lax.ppermute(array, axis, [(i, i ^ flip) for i in range(lax.axis_size(axi...  13.4 us
    pallas_call x2, Pallas kernels, attend(): pl.pallas_call(functools.partial(kernel, heads, dense), out_shape=out_sha...  2.91 us
    unnamed x7, local copies, waits for them, and re-layouts  2.25 us
    concatenate x1, local copies, waits for them, and re-layouts, per_device(): jnp.concatenate([keys.reshape(shape), values.reshape(shape)], axis=1)  0.77 us
    pallas_call x1, Pallas kernels, per_device(): pl.pallas_call(functools.partial(prepare_kernel, per, places, dense), out...  0.66 us
  transfers between devices with their start and end apart: 11, of which 0 were waited for; matrix products, arithmetic and copies ran while one was open for 0% of the time, Pallas kernels for 12%

commit v1 on v0

--- a/solution.py
+++ b/solution.py
@@ -304,7 +304,8 @@
         name="prepare",
     )(block_list, block_count)
     (far,), order = together([far], order)
-    last = across(far, cols) + across(opposite, cols)
+    far_across, queries = together(across(far, cols), queries)
+    last = far_across + across(opposite, cols)
     halves = [join_pieces([own, *own_across]), join_pieces([near, *near_across]), join_pieces([far, opposite])]
     early = join_pieces(halves + [swap(half, "col", 1) for half in halves], False)
 

time: 20.9 us -> 19.7 us (0.943)
  the two profiles are of different devices: /device:TPU:21 before, /device:TPU:0 now
where the time goes in v1:
time: 19.7 us; the launch traced here: 19.5 us
  starting transfers between devices  10.9 us (55%)
  waiting for transfers between devices  4.33 us (22%)
  Pallas kernels  3.36 us (17%)
  local copies, waits for them, and re-layouts  0.8 us (4%)
    ppermute x11, starting transfers between devices, swap(): lax.ppermute(array, axis, [(i, i ^ flip) for i in range(lax.axis_size(axi...  10.9 us
    ppermute x11, waiting for transfers between devices, swap(): lax.ppermute(array, axis, [(i, i ^ flip) for i in range(lax.axis_size(axi...  4.33 us
    pallas_call x2, Pallas kernels, attend(): pl.pallas_call(functools.partial(kernel, heads, dense), out_shape=out_sha...  2.27 us
    unnamed x9, local copies, waits for them, and re-layouts  0.79 us
    pallas_call x1, Pallas kernels, per_device(): pl.pallas_call(functools.partial(prepare_kernel, per, places, dense), out...  0.66 us
  transfers between devices with their start and end apart: 11, of which 3 were waited for; matrix products, arithmetic and copies ran while one was open for 0% of the time, Pallas kernels for 13%

profile of v1, /device:TPU:0, one launch (start us, length us, event | category | flops | bytes accessed | tf_op | source)
XLA Modules:
  0.0 19.5 jit_solution(17560651272154652543)
XLA Ops:
  0.0 0.8 %constant_dynamic-update-slice_fusion.1 = bf16[1,256,128]{2,1,0:T(8,128)(2,1)S(1)} fusion(bf16[1,128,128]{2,1,0:T(8,128)(2,1)} %param.6), kind=kLoop, calls=%fused_computation.1 | loop fusion | bytes 65536
  0.8 0.0 copy-done.3
  0.8 3.0 %collective-permute-start.5 = (bf16[1,256,128]{2,1,0:T(8,128)(2,1)S(1)}, bf16[1,256,128]{2,1,0:T(8,128)(2,1)S(1)}, u32[]{:S(2)}, u32[]{:S(2)}) collective-permute-start(bf16[1,256,128]{2,1,0:T(8,128)(2,1)S(1)} %constant_dynamic-update-slice_fusion.refs_0_), channel_id=1, source_target_pairs={{0,2},{1,3},{2,0},{3,1},{4,6},{5,7},{6,4},{7,5},{8,10},{9,11},{10,... | collective-permute-start | bytes 196616 | tf_op jit(solution)/shard_map/ppermute | solution.py:222
  3.8 2.6 %collective-permute-start = (bf16[1,256,128]{2,1,0:T(8,128)(2,1)S(1)}, bf16[1,256,128]{2,1,0:T(8,128)(2,1)S(1)}, u32[]{:S(2)}, u32[]{:S(2)}) collective-permute-start(bf16[1,256,128]{2,1,0:T(8,128)(2,1)S(1)} %constant_dynamic-update-slice_fusion.refs_0_), channel_id=1, source_target_pairs={{0,8},{4,12},{8,0},{12,4},{1,9},{5,13},{9,1},{13,5},{2,10},{6,14},... | collective-permute-start | bytes 196616 | tf_op jit(solution)/shard_map/ppermute | solution.py:222
  6.4 1.3 %collective-permute-start.2 = (bf16[1,256,128]{2,1,0:T(8,128)(2,1)S(1)}, bf16[1,256,128]{2,1,0:T(8,128)(2,1)S(1)}, u32[]{:S(2)}, u32[]{:S(2)}) collective-permute-start(bf16[1,256,128]{2,1,0:T(8,128)(2,1)S(1)} %constant_dynamic-update-slice_fusion.refs_0_), channel_id=1, source_target_pairs={{0,12},{4,8},{8,4},{12,0},{1,13},{5,9},{9,5},{13,1},{2,14},{6,10},... | collective-permute-start | bytes 196616 | tf_op jit(solution)/shard_map/ppermute | solution.py:222
  7.7 0.2 %collective-permute-start.6 = (bf16[1,256,128]{2,1,0:T(8,128)(2,1)S(1)}, bf16[1,256,128]{2,1,0:T(8,128)(2,1)S(1)}, u32[]{:S(2)}, u32[]{:S(2)}) collective-permute-start(bf16[1,256,128]{2,1,0:T(8,128)(2,1)S(1)} %constant_dynamic-update-slice_fusion.refs_0_), channel_id=1, source_target_pairs={{0,4},{4,0},{8,12},{12,8},{1,5},{5,1},{9,13},{13,9},{2,6},{6,2},{1... | collective-permute-start | bytes 196616 | tf_op jit(solution)/shard_map/ppermute | solution.py:222
  8.0 0.7 %prepare.1.order_in = s32[1,2,12,512]{3,2,1,0:T(8,128)S(1)} custom-call(s32[4,4,4,4]{3,2,1,0:T(4,128)S(1)} %copy-done.1, s32[4,4,4]{2,1,0:T(4,128)S(1)} %copy-done.2), custom_call_target="tpu_custom_call" | custom-call | tf_op jit(solution)/shard_map/prepare/pallas_call | solution.py:292
  8.6 0.0 collective-permute-done.5.refs_1_
  8.7 1.9 %collective-permute-start.7 = (bf16[1,256,128]{2,1,0:T(8,128)(2,1)S(1)}, bf16[1,256,128]{2,1,0:T(8,128)(2,1)S(1)}, u32[]{:S(2)}, u32[]{:S(2)}) collective-permute-start(bf16[1,256,128]{2,1,0:T(8,128)(2,1)S(1)} %collective-permute-done.5.refs_1_), channel_id=1, source_target_pairs={{0,4},{4,0},{8,12},{12,8},{1,5},{5,1},{9,13},{13,9},{2,6},{6,2},{1... | collective-permute-start | bytes 196616 | tf_op jit(solution)/shard_map/ppermute | solution.py:222
  10.5 0.0 collective-permute-done.refs_0_
  10.5 0.5 %collective-permute-start.1 = (bf16[1,256,128]{2,1,0:T(8,128)(2,1)S(1)}, bf16[1,256,128]{2,1,0:T(8,128)(2,1)S(1)}, u32[]{:S(2)}, u32[]{:S(2)}) collective-permute-start(bf16[1,256,128]{2,1,0:T(8,128)(2,1)S(1)} %collective-permute-done.refs_0_), channel_id=1, source_target_pairs={{0,2},{1,3},{2,0},{3,1},{4,6},{5,7},{6,4},{7,5},{8,10},{9,11},{10,... | collective-permute-start | bytes 196616 | tf_op jit(solution)/shard_map/ppermute | solution.py:222
  11.1 1.7 %collective-permute-done.2.refs_1_ = bf16[1,256,128]{2,1,0:T(8,128)(2,1)S(1)} collective-permute-done((bf16[1,256,128]{2,1,0:T(8,128)(2,1)S(1)}, bf16[1,256,128]{2,1,0:T(8,128)(2,1)S(1)}, u32[]{:S(2)}, u32[]{:S(2)}) %collective-permute-start.2) | collective-permute-done | bytes 65568 | tf_op jit(solution)/shard_map/ppermute | solution.py:222
  12.7 0.5 %collective-permute-start.3 = (bf16[1,256,128]{2,1,0:T(8,128)(2,1)S(1)}, bf16[1,256,128]{2,1,0:T(8,128)(2,1)S(1)}, u32[]{:S(2)}, u32[]{:S(2)}) collective-permute-start(bf16[1,256,128]{2,1,0:T(8,128)(2,1)S(1)} %collective-permute-done.2.refs_1_), channel_id=1, source_target_pairs={{0,2},{1,3},{2,0},{3,1},{4,6},{5,7},{6,4},{7,5},{8,10},{9,11},{10,... | collective-permute-start | bytes 196616 | tf_op jit(solution)/shard_map/ppermute | solution.py:222
  13.2 0.1 join.9.refs_2_
  13.3 0.1 collective-permute-start.10
  13.4 0.1 join.7.refs_0_
  13.5 0.0 copy-start
  13.5 0.0 collective-permute-done.6.refs_0_
  13.5 0.6 %collective-permute-start.8 = (bf16[2,256,128]{2,1,0:T(8,128)(2,1)S(1)}, bf16[2,256,128]{2,1,0:T(8,128)(2,1)S(1)}, u32[]{:S(2)}, u32[]{:S(2)}) collective-permute-start(bf16[2,256,128]{2,1,0:T(8,128)(2,1)S(1)} %join.7.refs_0_), channel_id=1, source_target_pairs={{0,1},{1,0},{2,3},{3,2},{4,5},{5,4},{6,7},{7,6},{8,9},{9,8},{10,11... | collective-permute-start | bytes 393224 | tf_op jit(solution)/shard_map/ppermute | solution.py:222
  14.1 0.0 collective-permute-done.7.refs_1_
  14.1 0.1 join.8.refs_1_
  14.1 0.1 collective-permute-start.9
  14.2 0.5 %collective-permute-done.1.refs_0_ = bf16[1,256,128]{2,1,0:T(8,128)(2,1)S(1)} collective-permute-done((bf16[1,256,128]{2,1,0:T(8,128)(2,1)S(1)}, bf16[1,256,128]{2,1,0:T(8,128)(2,1)S(1)}, u32[]{:S(2)}, u32[]{:S(2)}) %collective-permute-start.1) | collective-permute-done | bytes 65568 | tf_op jit(solution)/shard_map/ppermute | solution.py:222
  14.8 0.1 turn.1.qt_ref
  14.9 2.1 %collective-permute-done.3.refs_1_ = bf16[1,256,128]{2,1,0:T(8,128)(2,1)S(1)} collective-permute-done((bf16[1,256,128]{2,1,0:T(8,128)(2,1)S(1)}, bf16[1,256,128]{2,1,0:T(8,128)(2,1)S(1)}, u32[]{:S(2)}, u32[]{:S(2)}) %collective-permute-start.3) | collective-permute-done | bytes 65568 | tf_op jit(solution)/shard_map/ppermute | solution.py:222
  17.0 0.1 join.6.refs_0_
  17.1 0.1 collective-permute-start.4
  17.2 0.0 collective-permute-done.9.refs_4_
  17.2 0.1 join.10.kv_ref
  17.2 1.5 %early.1 = (f32[1,128,512]{2,1,0:T(8,128)S(1)}, f32[1,2,512]{2,1,0:T(2,128)S(1)}) custom-call(bf16[1,128,512]{2,1,0:T(8,128)(2,1)S(1)} %turn.1.qt_ref, s32[1,2,12,512]{3,2,1,0:T(8,128)S(1)} %prepare.1.order_in, bf16[12,256,128]{2,1,0:T(8,128)(2,1)S(1)} %join.10.kv_ref), custom_call_target="tpu_custom_call" | custom-call | tf_op jit(solution)/shard_map/early/pallas_call | solution.py:320
  18.7 0.0 collective-permute-done.4.refs_1_
  18.8 0.8 %last.1 = bf16[1,128,512]{2,1,0:T(8,128)(2,1)} custom-call(bf16[1,128,512]{2,1,0:T(8,128)(2,1)S(1)} %turn.1.qt_ref, s32[1,2,12,512]{3,2,1,0:T(8,128)S(1)} %prepare.1.order_in, bf16[4,256,128]{2,1,0:T(8,128)(2,1)S(1)} %join.11.kv_ref, f32[1,128,512]{2,1,0:T(8,128)S(1)} %get-tuple-element.27.acc_in, f32[1,2,512]{2,1,0:T(2,128)S(1)} %get-tuple-element.28.stats_in), custom_call_target="tpu_custom_call" | custom-call | tf_op jit(solution)/shard_map/last/pallas_call | solution.py:320
  (10 shorter events, 0.0 us)
Async XLA Ops:
  0.0 0.8 %copy-start.3 = (bf16[1,128,128]{2,1,0:T(8,128)(2,1)S(1)}, bf16[1,128,128]{2,1,0:T(8,128)(2,1)}, u32[]{:S(2)}) copy-start(bf16[1,128,128]{2,1,0:T(8,128)(2,1)} %param.7) | copy-start | bytes 98308
  0.8 7.2 %copy-start.1 = (s32[4,4,4,4]{3,2,1,0:T(4,128)S(1)}, s32[4,4,4,4]{3,2,1,0:T(4,128)}, u32[]{:S(2)}) copy-start(s32[4,4,4,4]{3,2,1,0:T(4,128)} %list_hbm.1) | copy-start | bytes 3076
  0.8 7.2 %copy-start.2 = (s32[4,4,4]{2,1,0:T(4,128)S(1)}, s32[4,4,4]{2,1,0:T(4,128)}, u32[]{:S(2)}) copy-start(s32[4,4,4]{2,1,0:T(4,128)} %count_hbm.1) | copy-start | bytes 772
  0.8 7.8 %collective-permute-start.5 = (bf16[1,256,128]{2,1,0:T(8,128)(2,1)S(1)}, bf16[1,256,128]{2,1,0:T(8,128)(2,1)S(1)}, u32[]{:S(2)}, u32[]{:S(2)}) collective-permute-start(bf16[1,256,128]{2,1,0:T(8,128)(2,1)S(1)} %constant_dynamic-update-slice_fusion.refs_0_), channel_id=1, source_target_pairs={{0,2},{1,3},{2,0},{3,1},{4,6},{5,7},{6,4},{7,5},{8,10},{9,11},{10,... | collective-permute-start | bytes 196616 | tf_op jit(solution)/shard_map/ppermute | solution.py:222
  3.8 6.7 %collective-permute-start = (bf16[1,256,128]{2,1,0:T(8,128)(2,1)S(1)}, bf16[1,256,128]{2,1,0:T(8,128)(2,1)S(1)}, u32[]{:S(2)}, u32[]{:S(2)}) collective-permute-start(bf16[1,256,128]{2,1,0:T(8,128)(2,1)S(1)} %constant_dynamic-update-slice_fusion.refs_0_), channel_id=1, source_target_pairs={{0,8},{4,12},{8,0},{12,4},{1,9},{5,13},{9,1},{13,5},{2,10},{6,14},... | collective-permute-start | bytes 196616 | tf_op jit(solution)/shard_map/ppermute | solution.py:222
  6.4 6.3 %collective-permute-start.2 = (bf16[1,256,128]{2,1,0:T(8,128)(2,1)S(1)}, bf16[1,256,128]{2,1,0:T(8,128)(2,1)S(1)}, u32[]{:S(2)}, u32[]{:S(2)}) collective-permute-start(bf16[1,256,128]{2,1,0:T(8,128)(2,1)S(1)} %constant_dynamic-update-slice_fusion.refs_0_), channel_id=1, source_target_pairs={{0,12},{4,8},{8,4},{12,0},{1,13},{5,9},{9,5},{13,1},{2,14},{6,10},... | collective-permute-start | bytes 196616 | tf_op jit(solution)/shard_map/ppermute | solution.py:222
  7.7 5.8 %collective-permute-start.6 = (bf16[1,256,128]{2,1,0:T(8,128)(2,1)S(1)}, bf16[1,256,128]{2,1,0:T(8,128)(2,1)S(1)}, u32[]{:S(2)}, u32[]{:S(2)}) collective-permute-start(bf16[1,256,128]{2,1,0:T(8,128)(2,1)S(1)} %constant_dynamic-update-slice_fusion.refs_0_), channel_id=1, source_target_pairs={{0,4},{4,0},{8,12},{12,8},{1,5},{5,1},{9,13},{13,9},{2,6},{6,2},{1... | collective-permute-start | bytes 196616 | tf_op jit(solution)/shard_map/ppermute | solution.py:222
  8.7 5.4 %collective-permute-start.7 = (bf16[1,256,128]{2,1,0:T(8,128)(2,1)S(1)}, bf16[1,256,128]{2,1,0:T(8,128)(2,1)S(1)}, u32[]{:S(2)}, u32[]{:S(2)}) collective-permute-start(bf16[1,256,128]{2,1,0:T(8,128)(2,1)S(1)} %collective-permute-done.5.refs_1_), channel_id=1, source_target_pairs={{0,4},{4,0},{8,12},{12,8},{1,5},{5,1},{9,13},{13,9},{2,6},{6,2},{1... | collective-permute-start | bytes 196616 | tf_op jit(solution)/shard_map/ppermute | solution.py:222
  10.5 4.3 %collective-permute-start.1 = (bf16[1,256,128]{2,1,0:T(8,128)(2,1)S(1)}, bf16[1,256,128]{2,1,0:T(8,128)(2,1)S(1)}, u32[]{:S(2)}, u32[]{:S(2)}) collective-permute-start(bf16[1,256,128]{2,1,0:T(8,128)(2,1)S(1)} %collective-permute-done.refs_0_), channel_id=1, source_target_pairs={{0,2},{1,3},{2,0},{3,1},{4,6},{5,7},{6,4},{7,5},{8,10},{9,11},{10,... | collective-permute-start | bytes 196616 | tf_op jit(solution)/shard_map/ppermute | solution.py:222
  12.7 4.3 %collective-permute-start.3 = (bf16[1,256,128]{2,1,0:T(8,128)(2,1)S(1)}, bf16[1,256,128]{2,1,0:T(8,128)(2,1)S(1)}, u32[]{:S(2)}, u32[]{:S(2)}) collective-permute-start(bf16[1,256,128]{2,1,0:T(8,128)(2,1)S(1)} %collective-permute-done.2.refs_1_), channel_id=1, source_target_pairs={{0,2},{1,3},{2,0},{3,1},{4,6},{5,7},{6,4},{7,5},{8,10},{9,11},{10,... | collective-permute-start | bytes 196616 | tf_op jit(solution)/shard_map/ppermute | solution.py:222
  13.3 3.8 %collective-permute-start.10 = (bf16[2,256,128]{2,1,0:T(8,128)(2,1)S(1)}, bf16[2,256,128]{2,1,0:T(8,128)(2,1)S(1)}, u32[]{:S(2)}, u32[]{:S(2)}) collective-permute-start(bf16[2,256,128]{2,1,0:T(8,128)(2,1)S(1)} %join.9.refs_2_), channel_id=1, source_target_pairs={{0,1},{1,0},{2,3},{3,2},{4,5},{5,4},{6,7},{7,6},{8,9},{9,8},{10,11... | collective-permute-start | bytes 393224 | tf_op jit(solution)/shard_map/ppermute | solution.py:222
  13.5 1.3 %copy-start = (bf16[1,128,512]{2,1,0:T(8,128)(2,1)S(1)}, bf16[1,128,512]{2,1,0:T(8,128)(2,1)}, u32[]{:S(2)}) copy-start(bf16[1,128,512]{2,1,0:T(8,128)(2,1)} %q_ref) | copy-start | bytes 393220
  13.5 3.6 %collective-permute-start.8 = (bf16[2,256,128]{2,1,0:T(8,128)(2,1)S(1)}, bf16[2,256,128]{2,1,0:T(8,128)(2,1)S(1)}, u32[]{:S(2)}, u32[]{:S(2)}) collective-permute-start(bf16[2,256,128]{2,1,0:T(8,128)(2,1)S(1)} %join.7.refs_0_), channel_id=1, source_target_pairs={{0,1},{1,0},{2,3},{3,2},{4,5},{5,4},{6,7},{7,6},{8,9},{9,8},{10,11... | collective-permute-start | bytes 393224 | tf_op jit(solution)/shard_map/ppermute | solution.py:222
  14.1 3.0 %collective-permute-start.9 = (bf16[2,256,128]{2,1,0:T(8,128)(2,1)S(1)}, bf16[2,256,128]{2,1,0:T(8,128)(2,1)S(1)}, u32[]{:S(2)}, u32[]{:S(2)}) collective-permute-start(bf16[2,256,128]{2,1,0:T(8,128)(2,1)S(1)} %join.8.refs_1_), channel_id=1, source_target_pairs={{0,1},{1,0},{2,3},{3,2},{4,5},{5,4},{6,7},{7,6},{8,9},{9,8},{10,11... | collective-permute-start | bytes 393224 | tf_op jit(solution)/shard_map/ppermute | solution.py:222
  17.1 1.7 %collective-permute-start.4 = (bf16[2,256,128]{2,1,0:T(8,128)(2,1)S(1)}, bf16[2,256,128]{2,1,0:T(8,128)(2,1)S(1)}, u32[]{:S(2)}, u32[]{:S(2)}) collective-permute-start(bf16[2,256,128]{2,1,0:T(8,128)(2,1)S(1)} %join.6.refs_0_), channel_id=1, source_target_pairs={{0,1},{1,0},{2,3},{3,2},{4,5},{5,4},{6,7},{7,6},{8,9},{9,8},{10,11... | collective-permute-start | bytes 393224 | tf_op jit(solution)/shard_map/ppermute | solution.py:222

commit v2 on v1

--- a/solution.py
+++ b/solution.py
@@ -303,8 +303,7 @@
         compiler_params=small,
         name="prepare",
     )(block_list, block_count)
-    (far,), order = together([far], order)
-    far_across, queries = together(across(far, cols), queries)
+    far_across, queries, order = together(across(far, cols), queries, order)
     last = far_across + across(opposite, cols)
     halves = [join_pieces([own, *own_across]), join_pieces([near, *near_across]), join_pieces([far, opposite])]
     early = join_pieces(halves + [swap(half, "col", 1) for half in halves], False)

time: 19.7 us -> 20 us (1.015)
  transfers between devices with their start and end apart: 11 -> 11, of which waited for: 3 -> 2; matrix products, arithmetic and copies ran while one was open for 0% -> 0% of each run, Pallas kernels for 13% -> 13%
where the time goes in v2:
time: 20 us; the launch traced here: 19.8 us
  starting transfers between devices  10.8 us (54%)
  waiting for transfers between devices  4.49 us (22%)
  Pallas kernels  3.36 us (17%)
  local copies, waits for them, and re-layouts  0.95 us (5%)
    ppermute x11, starting transfers between devices, swap(): lax.ppermute(array, axis, [(i, i ^ flip) for i in range(lax.axis_size(axi...  10.8 us
    ppermute x11, waiting for transfers between devices, swap(): lax.ppermute(array, axis, [(i, i ^ flip) for i in range(lax.axis_size(axi...  4.49 us
    pallas_call x2, Pallas kernels, attend(): pl.pallas_call(functools.partial(kernel, heads, dense), out_shape=out_sha...  2.27 us
    unnamed x9, local copies, waits for them, and re-layouts  0.94 us
    pallas_call x1, Pallas kernels, per_device(): pl.pallas_call(functools.partial(prepare_kernel, per, places, dense), out...  0.66 us
  transfers between devices with their start and end apart: 11, of which 2 were waited for; matrix products, arithmetic and copies ran while one was open for 0% of the time, Pallas kernels for 13%

profile of v2, /device:TPU:0, one launch (start us, length us, event | category | flops | bytes accessed | tf_op | source)
XLA Modules:
  0.0 19.8 jit_solution(1702655333067502685)
XLA Ops:
  0.0 0.8 %constant_dynamic-update-slice_fusion.1 = bf16[1,256,128]{2,1,0:T(8,128)(2,1)S(1)} fusion(bf16[1,128,128]{2,1,0:T(8,128)(2,1)} %param.6), kind=kLoop, calls=%fused_computation.1 | loop fusion | bytes 65536
  0.8 0.0 copy-done.3
  0.8 3.0 %collective-permute-start.5 = (bf16[1,256,128]{2,1,0:T(8,128)(2,1)S(1)}, bf16[1,256,128]{2,1,0:T(8,128)(2,1)S(1)}, u32[]{:S(2)}, u32[]{:S(2)}) collective-permute-start(bf16[1,256,128]{2,1,0:T(8,128)(2,1)S(1)} %constant_dynamic-update-slice_fusion.refs_0_), channel_id=1, source_target_pairs={{0,2},{1,3},{2,0},{3,1},{4,6},{5,7},{6,4},{7,5},{8,10},{9,11},{10,... | collective-permute-start | bytes 196616 | tf_op jit(solution)/shard_map/ppermute | solution.py:222
  3.8 2.6 %collective-permute-start = (bf16[1,256,128]{2,1,0:T(8,128)(2,1)S(1)}, bf16[1,256,128]{2,1,0:T(8,128)(2,1)S(1)}, u32[]{:S(2)}, u32[]{:S(2)}) collective-permute-start(bf16[1,256,128]{2,1,0:T(8,128)(2,1)S(1)} %constant_dynamic-update-slice_fusion.refs_0_), channel_id=1, source_target_pairs={{0,8},{4,12},{8,0},{12,4},{1,9},{5,13},{9,1},{13,5},{2,10},{6,14},... | collective-permute-start | bytes 196616 | tf_op jit(solution)/shard_map/ppermute | solution.py:222
  6.4 1.3 %collective-permute-start.2 = (bf16[1,256,128]{2,1,0:T(8,128)(2,1)S(1)}, bf16[1,256,128]{2,1,0:T(8,128)(2,1)S(1)}, u32[]{:S(2)}, u32[]{:S(2)}) collective-permute-start(bf16[1,256,128]{2,1,0:T(8,128)(2,1)S(1)} %constant_dynamic-update-slice_fusion.refs_0_), channel_id=1, source_target_pairs={{0,12},{4,8},{8,4},{12,0},{1,13},{5,9},{9,5},{13,1},{2,14},{6,10},... | collective-permute-start | bytes 196616 | tf_op jit(solution)/shard_map/ppermute | solution.py:222
  7.7 0.2 %collective-permute-start.6 = (bf16[1,256,128]{2,1,0:T(8,128)(2,1)S(1)}, bf16[1,256,128]{2,1,0:T(8,128)(2,1)S(1)}, u32[]{:S(2)}, u32[]{:S(2)}) collective-permute-start(bf16[1,256,128]{2,1,0:T(8,128)(2,1)S(1)} %constant_dynamic-update-slice_fusion.refs_0_), channel_id=1, source_target_pairs={{0,4},{4,0},{8,12},{12,8},{1,5},{5,1},{9,13},{13,9},{2,6},{6,2},{1... | collective-permute-start | bytes 196616 | tf_op jit(solution)/shard_map/ppermute | solution.py:222
  8.0 0.0 collective-permute-done.5.refs_1_
  8.0 1.8 %collective-permute-start.7 = (bf16[1,256,128]{2,1,0:T(8,128)(2,1)S(1)}, bf16[1,256,128]{2,1,0:T(8,128)(2,1)S(1)}, u32[]{:S(2)}, u32[]{:S(2)}) collective-permute-start(bf16[1,256,128]{2,1,0:T(8,128)(2,1)S(1)} %collective-permute-done.5.refs_1_), channel_id=1, source_target_pairs={{0,4},{4,0},{8,12},{12,8},{1,5},{5,1},{9,13},{13,9},{2,6},{6,2},{1... | collective-permute-start | bytes 196616 | tf_op jit(solution)/shard_map/ppermute | solution.py:222
  9.8 0.5 %collective-permute-start.1 = (bf16[1,256,128]{2,1,0:T(8,128)(2,1)S(1)}, bf16[1,256,128]{2,1,0:T(8,128)(2,1)S(1)}, u32[]{:S(2)}, u32[]{:S(2)}) collective-permute-start(bf16[1,256,128]{2,1,0:T(8,128)(2,1)S(1)} %collective-permute-done.refs_0_), channel_id=1, source_target_pairs={{0,2},{1,3},{2,0},{3,1},{4,6},{5,7},{6,4},{7,5},{8,10},{9,11},{10,... | collective-permute-start | bytes 196616 | tf_op jit(solution)/shard_map/ppermute | solution.py:222
  10.3 2.6 %collective-permute-done.2.refs_1_ = bf16[1,256,128]{2,1,0:T(8,128)(2,1)S(1)} collective-permute-done((bf16[1,256,128]{2,1,0:T(8,128)(2,1)S(1)}, bf16[1,256,128]{2,1,0:T(8,128)(2,1)S(1)}, u32[]{:S(2)}, u32[]{:S(2)}) %collective-permute-start.2) | collective-permute-done | bytes 65568 | tf_op jit(solution)/shard_map/ppermute | solution.py:222
  13.0 0.5 %collective-permute-start.3 = (bf16[1,256,128]{2,1,0:T(8,128)(2,1)S(1)}, bf16[1,256,128]{2,1,0:T(8,128)(2,1)S(1)}, u32[]{:S(2)}, u32[]{:S(2)}) collective-permute-start(bf16[1,256,128]{2,1,0:T(8,128)(2,1)S(1)} %collective-permute-done.2.refs_1_), channel_id=1, source_target_pairs={{0,2},{1,3},{2,0},{3,1},{4,6},{5,7},{6,4},{7,5},{8,10},{9,11},{10,... | collective-permute-start | bytes 196616 | tf_op jit(solution)/shard_map/ppermute | solution.py:222
  13.5 0.7 %prepare.1.order_in = s32[1,2,12,512]{3,2,1,0:T(8,128)S(1)} custom-call(s32[4,4,4,4]{3,2,1,0:T(4,128)S(1)} %copy-done.1, s32[4,4,4]{2,1,0:T(4,128)S(1)} %copy-done.2), custom_call_target="tpu_custom_call" | custom-call | tf_op jit(solution)/shard_map/prepare/pallas_call | solution.py:292
  14.2 0.1 join.9.refs_2_
  14.2 0.1 collective-permute-start.10
  14.3 0.1 join.7.refs_0_
  14.4 0.0 copy-start
  14.4 0.6 %collective-permute-start.8 = (bf16[2,256,128]{2,1,0:T(8,128)(2,1)S(1)}, bf16[2,256,128]{2,1,0:T(8,128)(2,1)S(1)}, u32[]{:S(2)}, u32[]{:S(2)}) collective-permute-start(bf16[2,256,128]{2,1,0:T(8,128)(2,1)S(1)} %join.7.refs_0_), channel_id=1, source_target_pairs={{0,1},{1,0},{2,3},{3,2},{4,5},{5,4},{6,7},{7,6},{8,9},{9,8},{10,11... | collective-permute-start | bytes 393224 | tf_op jit(solution)/shard_map/ppermute | solution.py:222
  15.0 0.0 collective-permute-done.7.refs_1_
  15.0 0.1 join.8.refs_1_
  15.1 0.1 collective-permute-start.9
  15.2 0.0 collective-permute-done.1.refs_0_
  15.2 0.2 copy-done
  15.3 0.1 turn.1.qt_ref
  15.4 1.8 %collective-permute-done.3.refs_1_ = bf16[1,256,128]{2,1,0:T(8,128)(2,1)S(1)} collective-permute-done((bf16[1,256,128]{2,1,0:T(8,128)(2,1)S(1)}, bf16[1,256,128]{2,1,0:T(8,128)(2,1)S(1)}, u32[]{:S(2)}, u32[]{:S(2)}) %collective-permute-start.3) | collective-permute-done | bytes 65568 | tf_op jit(solution)/shard_map/ppermute | solution.py:222
  17.2 0.1 join.6.refs_0_
  17.3 0.1 collective-permute-start.4
  17.4 0.0 collective-permute-done.10.refs_5_
  17.4 0.0 collective-permute-done.9.refs_4_
  17.4 0.1 join.10.kv_ref
  17.5 1.5 %early.1 = (f32[1,128,512]{2,1,0:T(8,128)S(1)}, f32[1,2,512]{2,1,0:T(2,128)S(1)}) custom-call(bf16[1,128,512]{2,1,0:T(8,128)(2,1)S(1)} %turn.1.qt_ref, s32[1,2,12,512]{3,2,1,0:T(8,128)S(1)} %prepare.1.order_in, bf16[12,256,128]{2,1,0:T(8,128)(2,1)S(1)} %join.10.kv_ref), custom_call_target="tpu_custom_call" | custom-call | tf_op jit(solution)/shard_map/early/pallas_call | solution.py:319
  19.0 0.0 collective-permute-done.4.refs_1_
  19.0 0.8 %last.1 = bf16[1,128,512]{2,1,0:T(8,128)(2,1)} custom-call(bf16[1,128,512]{2,1,0:T(8,128)(2,1)S(1)} %turn.1.qt_ref, s32[1,2,12,512]{3,2,1,0:T(8,128)S(1)} %prepare.1.order_in, bf16[4,256,128]{2,1,0:T(8,128)(2,1)S(1)} %join.11.kv_ref, f32[1,128,512]{2,1,0:T(8,128)S(1)} %get-tuple-element.25.acc_in, f32[1,2,512]{2,1,0:T(2,128)S(1)} %get-tuple-element.26.stats_in), custom_call_target="tpu_custom_call" | custom-call | tf_op jit(solution)/shard_map/last/pallas_call | solution.py:319
  (10 shorter events, 0.0 us)
Async XLA Ops:
  0.0 0.8 %copy-start.3 = (bf16[1,128,128]{2,1,0:T(8,128)(2,1)S(1)}, bf16[1,128,128]{2,1,0:T(8,128)(2,1)}, u32[]{:S(2)}) copy-start(bf16[1,128,128]{2,1,0:T(8,128)(2,1)} %param.7) | copy-start | bytes 98308
  0.8 12.7 %copy-start.1 = (s32[4,4,4,4]{3,2,1,0:T(4,128)S(1)}, s32[4,4,4,4]{3,2,1,0:T(4,128)}, u32[]{:S(2)}) copy-start(s32[4,4,4,4]{3,2,1,0:T(4,128)} %list_hbm.1) | copy-start | bytes 3076
  0.8 12.7 %copy-start.2 = (s32[4,4,4]{2,1,0:T(4,128)S(1)}, s32[4,4,4]{2,1,0:T(4,128)}, u32[]{:S(2)}) copy-start(s32[4,4,4]{2,1,0:T(4,128)} %count_hbm.1) | copy-start | bytes 772
  0.8 7.2 %collective-permute-start.5 = (bf16[1,256,128]{2,1,0:T(8,128)(2,1)S(1)}, bf16[1,256,128]{2,1,0:T(8,128)(2,1)S(1)}, u32[]{:S(2)}, u32[]{:S(2)}) collective-permute-start(bf16[1,256,128]{2,1,0:T(8,128)(2,1)S(1)} %constant_dynamic-update-slice_fusion.refs_0_), channel_id=1, source_target_pairs={{0,2},{1,3},{2,0},{3,1},{4,6},{5,7},{6,4},{7,5},{8,10},{9,11},{10,... | collective-permute-start | bytes 196616 | tf_op jit(solution)/shard_map/ppermute | solution.py:222
  3.8 6.0 %collective-permute-start = (bf16[1,256,128]{2,1,0:T(8,128)(2,1)S(1)}, bf16[1,256,128]{2,1,0:T(8,128)(2,1)S(1)}, u32[]{:S(2)}, u32[]{:S(2)}) collective-permute-start(bf16[1,256,128]{2,1,0:T(8,128)(2,1)S(1)} %constant_dynamic-update-slice_fusion.refs_0_), channel_id=1, source_target_pairs={{0,8},{4,12},{8,0},{12,4},{1,9},{5,13},{9,1},{13,5},{2,10},{6,14},... | collective-permute-start | bytes 196616 | tf_op jit(solution)/shard_map/ppermute | solution.py:222
  6.4 6.6 %collective-permute-start.2 = (bf16[1,256,128]{2,1,0:T(8,128)(2,1)S(1)}, bf16[1,256,128]{2,1,0:T(8,128)(2,1)S(1)}, u32[]{:S(2)}, u32[]{:S(2)}) collective-permute-start(bf16[1,256,128]{2,1,0:T(8,128)(2,1)S(1)} %constant_dynamic-update-slice_fusion.refs_0_), channel_id=1, source_target_pairs={{0,12},{4,8},{8,4},{12,0},{1,13},{5,9},{9,5},{13,1},{2,14},{6,10},... | collective-permute-start | bytes 196616 | tf_op jit(solution)/shard_map/ppermute | solution.py:222
  7.7 6.7 %collective-permute-start.6 = (bf16[1,256,128]{2,1,0:T(8,128)(2,1)S(1)}, bf16[1,256,128]{2,1,0:T(8,128)(2,1)S(1)}, u32[]{:S(2)}, u32[]{:S(2)}) collective-permute-start(bf16[1,256,128]{2,1,0:T(8,128)(2,1)S(1)} %constant_dynamic-update-slice_fusion.refs_0_), channel_id=1, source_target_pairs={{0,4},{4,0},{8,12},{12,8},{1,5},{5,1},{9,13},{13,9},{2,6},{6,2},{1... | collective-permute-start | bytes 196616 | tf_op jit(solution)/shard_map/ppermute | solution.py:222
  8.0 7.0 %collective-permute-start.7 = (bf16[1,256,128]{2,1,0:T(8,128)(2,1)S(1)}, bf16[1,256,128]{2,1,0:T(8,128)(2,1)S(1)}, u32[]{:S(2)}, u32[]{:S(2)}) collective-permute-start(bf16[1,256,128]{2,1,0:T(8,128)(2,1)S(1)} %collective-permute-done.5.refs_1_), channel_id=1, source_target_pairs={{0,4},{4,0},{8,12},{12,8},{1,5},{5,1},{9,13},{13,9},{2,6},{6,2},{1... | collective-permute-start | bytes 196616 | tf_op jit(solution)/shard_map/ppermute | solution.py:222
  9.8 5.4 %collective-permute-start.1 = (bf16[1,256,128]{2,1,0:T(8,128)(2,1)S(1)}, bf16[1,256,128]{2,1,0:T(8,128)(2,1)S(1)}, u32[]{:S(2)}, u32[]{:S(2)}) collective-permute-start(bf16[1,256,128]{2,1,0:T(8,128)(2,1)S(1)} %collective-permute-done.refs_0_), channel_id=1, source_target_pairs={{0,2},{1,3},{2,0},{3,1},{4,6},{5,7},{6,4},{7,5},{8,10},{9,11},{10,... | collective-permute-start | bytes 196616 | tf_op jit(solution)/shard_map/ppermute | solution.py:222
  13.0 4.3 %collective-permute-start.3 = (bf16[1,256,128]{2,1,0:T(8,128)(2,1)S(1)}, bf16[1,256,128]{2,1,0:T(8,128)(2,1)S(1)}, u32[]{:S(2)}, u32[]{:S(2)}) collective-permute-start(bf16[1,256,128]{2,1,0:T(8,128)(2,1)S(1)} %collective-permute-done.2.refs_1_), channel_id=1, source_target_pairs={{0,2},{1,3},{2,0},{3,1},{4,6},{5,7},{6,4},{7,5},{8,10},{9,11},{10,... | collective-permute-start | bytes 196616 | tf_op jit(solution)/shard_map/ppermute | solution.py:222
  14.2 3.1 %collective-permute-start.10 = (bf16[2,256,128]{2,1,0:T(8,128)(2,1)S(1)}, bf16[2,256,128]{2,1,0:T(8,128)(2,1)S(1)}, u32[]{:S(2)}, u32[]{:S(2)}) collective-permute-start(bf16[2,256,128]{2,1,0:T(8,128)(2,1)S(1)} %join.9.refs_2_), channel_id=1, source_target_pairs={{0,1},{1,0},{2,3},{3,2},{4,5},{5,4},{6,7},{7,6},{8,9},{9,8},{10,11... | collective-permute-start | bytes 393224 | tf_op jit(solution)/shard_map/ppermute | solution.py:222
  14.4 0.9 %copy-start = (bf16[1,128,512]{2,1,0:T(8,128)(2,1)S(1)}, bf16[1,128,512]{2,1,0:T(8,128)(2,1)}, u32[]{:S(2)}) copy-start(bf16[1,128,512]{2,1,0:T(8,128)(2,1)} %q_ref) | copy-start | bytes 393220
  14.4 3.0 %collective-permute-start.8 = (bf16[2,256,128]{2,1,0:T(8,128)(2,1)S(1)}, bf16[2,256,128]{2,1,0:T(8,128)(2,1)S(1)}, u32[]{:S(2)}, u32[]{:S(2)}) collective-permute-start(bf16[2,256,128]{2,1,0:T(8,128)(2,1)S(1)} %join.7.refs_0_), channel_id=1, source_target_pairs={{0,1},{1,0},{2,3},{3,2},{4,5},{5,4},{6,7},{7,6},{8,9},{9,8},{10,11... | collective-permute-start | bytes 393224 | tf_op jit(solution)/shard_map/ppermute | solution.py:222
  15.1 2.3 %collective-permute-start.9 = (bf16[2,256,128]{2,1,0:T(8,128)(2,1)S(1)}, bf16[2,256,128]{2,1,0:T(8,128)(2,1)S(1)}, u32[]{:S(2)}, u32[]{:S(2)}) collective-permute-start(bf16[2,256,128]{2,1,0:T(8,128)(2,1)S(1)} %join.8.refs_1_), channel_id=1, source_target_pairs={{0,1},{1,0},{2,3},{3,2},{4,5},{5,4},{6,7},{7,6},{8,9},{9,8},{10,11... | collective-permute-start | bytes 393224 | tf_op jit(solution)/shard_map/ppermute | solution.py:222
  17.3 1.7 %collective-permute-start.4 = (bf16[2,256,128]{2,1,0:T(8,128)(2,1)S(1)}, bf16[2,256,128]{2,1,0:T(8,128)(2,1)S(1)}, u32[]{:S(2)}, u32[]{:S(2)}) collective-permute-start(bf16[2,256,128]{2,1,0:T(8,128)(2,1)S(1)} %join.6.refs_0_), channel_id=1, source_target_pairs={{0,1},{1,0},{2,3},{3,2},{4,5},{5,4},{6,7},{7,6},{8,9},{9,8},{10,11... | collective-permute-start | bytes 393224 | tf_op jit(solution)/shard_map/ppermute | solution.py:222

commit v3 on v2

--- a/solution.py
+++ b/solution.py
@@ -281,7 +281,7 @@
     near, far, opposite = (swap(own, "row", flip) for flip in (1, 2, 3))
     own_across = across(own, cols)
     near_across = [swap(piece, "row", 1) for piece in own_across]
-    early_places = [place for _, where in (own, *own_across, near, *near_across, far, opposite) for place in where]
+    early_places = [place for _, where in (own, near, *own_across, *near_across, far, opposite) for place in where]
     late_places = [(r, c ^ flip) for flip in range(CORES, cols, CORES) for r, c in far[1] + opposite[1]]
     places = [where + [(r, c ^ 1) for r, c in where] for where in (early_places, late_places)]
 
@@ -303,9 +303,13 @@
         compiler_params=small,
         name="prepare",
     )(block_list, block_count)
-    far_across, queries, order = together(across(far, cols), queries, order)
+    (far, near), order = together([far, near], order)
+    far_across = across(far, cols)
+    seconds = together(far_across + near_across)
+    far_across, near_across = seconds[: len(far_across)], seconds[len(far_across) :]
     last = far_across + across(opposite, cols)
-    halves = [join_pieces([own, *own_across]), join_pieces([near, *near_across]), join_pieces([far, opposite])]
+    last, queries = together(last, queries)
+    halves = [join_pieces([own, near]), join_pieces([*own_across, *near_across]), join_pieces([far, opposite])]
     early = join_pieces(halves + [swap(half, "col", 1) for half in halves], False)
 
     def attend(kernel, name, out_shape, out_specs, scratch, *args):
@@ -334,7 +338,6 @@
         compiler_params=small,
         name="turn",
     )(queries)
-    last, queries_across = together(last, queries_across)
     parts = (
         jax.ShapeDtypeStruct((own_blocks, head_size, width), jnp.float32),
         jax.ShapeDtypeStruct((own_blocks, 2, width), jnp.float32),

time: 20 us -> 21.5 us (1.075)
  starting transfers between devices: 10.8 us -> 12.2 us
  waiting for transfers between devices: 4.49 us -> 4.78 us
    ppermute x11, starting transfers between devices: 10.8 us -> 12.2 us  [swap(): lax.ppermute(array, axis, [(i, i ^ flip) for i in range(lax.axis_size(axi...]
    ppermute x11, waiting for transfers between devices: 4.49 us -> 4.78 us  [swap(): lax.ppermute(array, axis, [(i, i ^ flip) for i in range(lax.axis_size(axi...]
  transfers between devices with their start and end apart: 11 -> 11, of which waited for: 2 -> 4; matrix products, arithmetic and copies ran while one was open for 0% -> 0% of each run, Pallas kernels for 13% -> 12%
where the time goes in v3:
time: 21.5 us; the launch traced here: 21.3 us
  starting transfers between devices  12.2 us (57%)
  waiting for transfers between devices  4.78 us (22%)
  Pallas kernels  3.37 us (16%)
  local copies, waits for them, and re-layouts  0.8 us (4%)
    ppermute x11, starting transfers between devices, swap(): lax.ppermute(array, axis, [(i, i ^ flip) for i in range(lax.axis_size(axi...  12.2 us
    ppermute x11, waiting for transfers between devices, swap(): lax.ppermute(array, axis, [(i, i ^ flip) for i in range(lax.axis_size(axi...  4.78 us
    pallas_call x2, Pallas kernels, attend(): pl.pallas_call(functools.partial(kernel, heads, dense), out_shape=out_sha...  2.27 us
    unnamed x9, local copies, waits for them, and re-layouts  0.79 us
    pallas_call x1, Pallas kernels, per_device(): pl.pallas_call(functools.partial(prepare_kernel, per, places, dense), out...  0.66 us
  transfers between devices with their start and end apart: 11, of which 4 were waited for; matrix products, arithmetic and copies ran while one was open for 0% of the time, Pallas kernels for 12%

profile of v3, /device:TPU:0, one launch (start us, length us, event | category | flops | bytes accessed | tf_op | source)
XLA Modules:
  0.0 21.3 jit_solution(3516330659788259146)
XLA Ops:
  0.0 0.8 %constant_dynamic-update-slice_fusion.1 = bf16[1,256,128]{2,1,0:T(8,128)(2,1)S(1)} fusion(bf16[1,128,128]{2,1,0:T(8,128)(2,1)} %param.6), kind=kLoop, calls=%fused_computation.1 | loop fusion | bytes 65536
  0.8 0.0 copy-done.3
  0.8 4.1 %collective-permute-start = (bf16[1,256,128]{2,1,0:T(8,128)(2,1)S(1)}, bf16[1,256,128]{2,1,0:T(8,128)(2,1)S(1)}, u32[]{:S(2)}, u32[]{:S(2)}) collective-permute-start(bf16[1,256,128]{2,1,0:T(8,128)(2,1)S(1)} %constant_dynamic-update-slice_fusion.refs_0_), channel_id=1, source_target_pairs={{0,8},{4,12},{8,0},{12,4},{1,9},{5,13},{9,1},{13,5},{2,10},{6,14},... | collective-permute-start | bytes 196616 | tf_op jit(solution)/shard_map/ppermute | solution.py:222
  4.9 1.6 %collective-permute-start.1 = (bf16[1,256,128]{2,1,0:T(8,128)(2,1)S(1)}, bf16[1,256,128]{2,1,0:T(8,128)(2,1)S(1)}, u32[]{:S(2)}, u32[]{:S(2)}) collective-permute-start(bf16[1,256,128]{2,1,0:T(8,128)(2,1)S(1)} %constant_dynamic-update-slice_fusion.refs_0_), channel_id=1, source_target_pairs={{0,4},{4,0},{8,12},{12,8},{1,5},{5,1},{9,13},{13,9},{2,6},{6,2},{1... | collective-permute-start | bytes 196616 | tf_op jit(solution)/shard_map/ppermute | solution.py:222
  6.5 1.5 %collective-permute-start.3 = (bf16[1,256,128]{2,1,0:T(8,128)(2,1)S(1)}, bf16[1,256,128]{2,1,0:T(8,128)(2,1)S(1)}, u32[]{:S(2)}, u32[]{:S(2)}) collective-permute-start(bf16[1,256,128]{2,1,0:T(8,128)(2,1)S(1)} %constant_dynamic-update-slice_fusion.refs_0_), channel_id=1, source_target_pairs={{0,2},{1,3},{2,0},{3,1},{4,6},{5,7},{6,4},{7,5},{8,10},{9,11},{10,... | collective-permute-start | bytes 196616 | tf_op jit(solution)/shard_map/ppermute | solution.py:222
  8.0 0.2 %collective-permute-start.5 = (bf16[1,256,128]{2,1,0:T(8,128)(2,1)S(1)}, bf16[1,256,128]{2,1,0:T(8,128)(2,1)S(1)}, u32[]{:S(2)}, u32[]{:S(2)}) collective-permute-start(bf16[1,256,128]{2,1,0:T(8,128)(2,1)S(1)} %constant_dynamic-update-slice_fusion.refs_0_), channel_id=1, source_target_pairs={{0,12},{4,8},{8,4},{12,0},{1,13},{5,9},{9,5},{13,1},{2,14},{6,10},... | collective-permute-start | bytes 196616 | tf_op jit(solution)/shard_map/ppermute | solution.py:222
  8.2 0.7 %prepare.1.order_in = s32[1,2,12,512]{3,2,1,0:T(8,128)S(1)} custom-call(s32[4,4,4,4]{3,2,1,0:T(4,128)S(1)} %copy-done.1, s32[4,4,4]{2,1,0:T(4,128)S(1)} %copy-done.2), custom_call_target="tpu_custom_call" | custom-call | tf_op jit(solution)/shard_map/prepare/pallas_call | solution.py:292
  8.9 0.0 collective-permute-done.refs_0_
  8.9 0.3 %collective-permute-done.1.refs_1_ = bf16[1,256,128]{2,1,0:T(8,128)(2,1)S(1)} collective-permute-done((bf16[1,256,128]{2,1,0:T(8,128)(2,1)S(1)}, bf16[1,256,128]{2,1,0:T(8,128)(2,1)S(1)}, u32[]{:S(2)}, u32[]{:S(2)}) %collective-permute-start.1) | collective-permute-done | bytes 65568 | tf_op jit(solution)/shard_map/ppermute | solution.py:222
  9.2 1.5 %collective-permute-start.2 = (bf16[1,256,128]{2,1,0:T(8,128)(2,1)S(1)}, bf16[1,256,128]{2,1,0:T(8,128)(2,1)S(1)}, u32[]{:S(2)}, u32[]{:S(2)}) collective-permute-start(bf16[1,256,128]{2,1,0:T(8,128)(2,1)S(1)} %collective-permute-done.refs_0_), channel_id=1, source_target_pairs={{0,2},{1,3},{2,0},{3,1},{4,6},{5,7},{6,4},{7,5},{8,10},{9,11},{10,... | collective-permute-start | bytes 196616 | tf_op jit(solution)/shard_map/ppermute | solution.py:222
  10.7 0.1 collective-permute-done.3.refs_0_
  10.7 2.0 %collective-permute-start.4 = (bf16[1,256,128]{2,1,0:T(8,128)(2,1)S(1)}, bf16[1,256,128]{2,1,0:T(8,128)(2,1)S(1)}, u32[]{:S(2)}, u32[]{:S(2)}) collective-permute-start(bf16[1,256,128]{2,1,0:T(8,128)(2,1)S(1)} %collective-permute-done.3.refs_0_), channel_id=1, source_target_pairs={{0,4},{4,0},{8,12},{12,8},{1,5},{5,1},{9,13},{13,9},{2,6},{6,2},{1... | collective-permute-start | bytes 196616 | tf_op jit(solution)/shard_map/ppermute | solution.py:222
  12.8 1.6 %collective-permute-done.5.refs_1_ = bf16[1,256,128]{2,1,0:T(8,128)(2,1)S(1)} collective-permute-done((bf16[1,256,128]{2,1,0:T(8,128)(2,1)S(1)}, bf16[1,256,128]{2,1,0:T(8,128)(2,1)S(1)}, u32[]{:S(2)}, u32[]{:S(2)}) %collective-permute-start.5) | collective-permute-done | bytes 65568 | tf_op jit(solution)/shard_map/ppermute | solution.py:222
  14.4 0.5 %collective-permute-start.6 = (bf16[1,256,128]{2,1,0:T(8,128)(2,1)S(1)}, bf16[1,256,128]{2,1,0:T(8,128)(2,1)S(1)}, u32[]{:S(2)}, u32[]{:S(2)}) collective-permute-start(bf16[1,256,128]{2,1,0:T(8,128)(2,1)S(1)} %collective-permute-done.5.refs_1_), channel_id=1, source_target_pairs={{0,2},{1,3},{2,0},{3,1},{4,6},{5,7},{6,4},{7,5},{8,10},{9,11},{10,... | collective-permute-start | bytes 196616 | tf_op jit(solution)/shard_map/ppermute | solution.py:222
  14.9 0.1 join.9.refs_2_
  15.0 0.1 collective-permute-start.10
  15.1 0.1 join.7.refs_0_
  15.2 0.6 %collective-permute-start.8 = (bf16[2,256,128]{2,1,0:T(8,128)(2,1)S(1)}, bf16[2,256,128]{2,1,0:T(8,128)(2,1)S(1)}, u32[]{:S(2)}, u32[]{:S(2)}) collective-permute-start(bf16[2,256,128]{2,1,0:T(8,128)(2,1)S(1)} %join.7.refs_0_), channel_id=1, source_target_pairs={{0,1},{1,0},{2,3},{3,2},{4,5},{5,4},{6,7},{7,6},{8,9},{9,8},{10,11... | collective-permute-start | bytes 393224 | tf_op jit(solution)/shard_map/ppermute | solution.py:222
  15.7 0.0 collective-permute-done.2.refs_0_
  15.7 0.1 join.8.refs_1_
  15.8 0.0 copy-start
  15.8 0.1 collective-permute-start.9
  15.9 2.7 %collective-permute-done.6.refs_1_ = bf16[1,256,128]{2,1,0:T(8,128)(2,1)S(1)} collective-permute-done((bf16[1,256,128]{2,1,0:T(8,128)(2,1)S(1)}, bf16[1,256,128]{2,1,0:T(8,128)(2,1)S(1)}, u32[]{:S(2)}, u32[]{:S(2)}) %collective-permute-start.6) | collective-permute-done | bytes 65568 | tf_op jit(solution)/shard_map/ppermute | solution.py:222
  18.7 0.1 join.6.refs_0_
  18.8 0.1 collective-permute-start.7
  18.8 0.1 turn.1.qt_ref
  18.9 0.0 collective-permute-done.8.refs_3_
  19.0 0.0 collective-permute-done.9.refs_4_
  19.0 0.1 join.10.kv_ref
  19.0 1.5 %early.1 = (f32[1,128,512]{2,1,0:T(8,128)S(1)}, f32[1,2,512]{2,1,0:T(2,128)S(1)}) custom-call(bf16[1,128,512]{2,1,0:T(8,128)(2,1)S(1)} %turn.1.qt_ref, s32[1,2,12,512]{3,2,1,0:T(8,128)S(1)} %prepare.1.order_in, bf16[12,256,128]{2,1,0:T(8,128)(2,1)S(1)} %join.10.kv_ref), custom_call_target="tpu_custom_call" | custom-call | tf_op jit(solution)/shard_map/early/pallas_call | solution.py:323
  20.5 0.0 collective-permute-done.7.refs_1_
  20.6 0.8 %last.1 = bf16[1,128,512]{2,1,0:T(8,128)(2,1)} custom-call(bf16[1,128,512]{2,1,0:T(8,128)(2,1)S(1)} %turn.1.qt_ref, s32[1,2,12,512]{3,2,1,0:T(8,128)S(1)} %prepare.1.order_in, bf16[4,256,128]{2,1,0:T(8,128)(2,1)S(1)} %join.11.kv_ref, f32[1,128,512]{2,1,0:T(8,128)S(1)} %get-tuple-element.29.acc_in, f32[1,2,512]{2,1,0:T(2,128)S(1)} %get-tuple-element.30.stats_in), custom_call_target="tpu_custom_call" | custom-call | tf_op jit(solution)/shard_map/last/pallas_call | solution.py:323
  (10 shorter events, 0.0 us)
Async XLA Ops:
  0.0 0.8 %copy-start.3 = (bf16[1,128,128]{2,1,0:T(8,128)(2,1)S(1)}, bf16[1,128,128]{2,1,0:T(8,128)(2,1)}, u32[]{:S(2)}) copy-start(bf16[1,128,128]{2,1,0:T(8,128)(2,1)} %param.7) | copy-start | bytes 98308
  0.8 7.4 %copy-start.1 = (s32[4,4,4,4]{3,2,1,0:T(4,128)S(1)}, s32[4,4,4,4]{3,2,1,0:T(4,128)}, u32[]{:S(2)}) copy-start(s32[4,4,4,4]{3,2,1,0:T(4,128)} %list_hbm.1) | copy-start | bytes 3076
  0.8 7.4 %copy-start.2 = (s32[4,4,4]{2,1,0:T(4,128)S(1)}, s32[4,4,4]{2,1,0:T(4,128)}, u32[]{:S(2)}) copy-start(s32[4,4,4]{2,1,0:T(4,128)} %count_hbm.1) | copy-start | bytes 772
  0.8 8.1 %collective-permute-start = (bf16[1,256,128]{2,1,0:T(8,128)(2,1)S(1)}, bf16[1,256,128]{2,1,0:T(8,128)(2,1)S(1)}, u32[]{:S(2)}, u32[]{:S(2)}) collective-permute-start(bf16[1,256,128]{2,1,0:T(8,128)(2,1)S(1)} %constant_dynamic-update-slice_fusion.refs_0_), channel_id=1, source_target_pairs={{0,8},{4,12},{8,0},{12,4},{1,9},{5,13},{9,1},{13,5},{2,10},{6,14},... | collective-permute-start | bytes 196616 | tf_op jit(solution)/shard_map/ppermute | solution.py:222
  4.9 4.3 %collective-permute-start.1 = (bf16[1,256,128]{2,1,0:T(8,128)(2,1)S(1)}, bf16[1,256,128]{2,1,0:T(8,128)(2,1)S(1)}, u32[]{:S(2)}, u32[]{:S(2)}) collective-permute-start(bf16[1,256,128]{2,1,0:T(8,128)(2,1)S(1)} %constant_dynamic-update-slice_fusion.refs_0_), channel_id=1, source_target_pairs={{0,4},{4,0},{8,12},{12,8},{1,5},{5,1},{9,13},{13,9},{2,6},{6,2},{1... | collective-permute-start | bytes 196616 | tf_op jit(solution)/shard_map/ppermute | solution.py:222
  6.5 4.3 %collective-permute-start.3 = (bf16[1,256,128]{2,1,0:T(8,128)(2,1)S(1)}, bf16[1,256,128]{2,1,0:T(8,128)(2,1)S(1)}, u32[]{:S(2)}, u32[]{:S(2)}) collective-permute-start(bf16[1,256,128]{2,1,0:T(8,128)(2,1)S(1)} %constant_dynamic-update-slice_fusion.refs_0_), channel_id=1, source_target_pairs={{0,2},{1,3},{2,0},{3,1},{4,6},{5,7},{6,4},{7,5},{8,10},{9,11},{10,... | collective-permute-start | bytes 196616 | tf_op jit(solution)/shard_map/ppermute | solution.py:222
  8.0 6.4 %collective-permute-start.5 = (bf16[1,256,128]{2,1,0:T(8,128)(2,1)S(1)}, bf16[1,256,128]{2,1,0:T(8,128)(2,1)S(1)}, u32[]{:S(2)}, u32[]{:S(2)}) collective-permute-start(bf16[1,256,128]{2,1,0:T(8,128)(2,1)S(1)} %constant_dynamic-update-slice_fusion.refs_0_), channel_id=1, source_target_pairs={{0,12},{4,8},{8,4},{12,0},{1,13},{5,9},{9,5},{13,1},{2,14},{6,10},... | collective-permute-start | bytes 196616 | tf_op jit(solution)/shard_map/ppermute | solution.py:222
  9.2 6.6 %collective-permute-start.2 = (bf16[1,256,128]{2,1,0:T(8,128)(2,1)S(1)}, bf16[1,256,128]{2,1,0:T(8,128)(2,1)S(1)}, u32[]{:S(2)}, u32[]{:S(2)}) collective-permute-start(bf16[1,256,128]{2,1,0:T(8,128)(2,1)S(1)} %collective-permute-done.refs_0_), channel_id=1, source_target_pairs={{0,2},{1,3},{2,0},{3,1},{4,6},{5,7},{6,4},{7,5},{8,10},{9,11},{10,... | collective-permute-start | bytes 196616 | tf_op jit(solution)/shard_map/ppermute | solution.py:222
  10.7 5.0 %collective-permute-start.4 = (bf16[1,256,128]{2,1,0:T(8,128)(2,1)S(1)}, bf16[1,256,128]{2,1,0:T(8,128)(2,1)S(1)}, u32[]{:S(2)}, u32[]{:S(2)}) collective-permute-start(bf16[1,256,128]{2,1,0:T(8,128)(2,1)S(1)} %collective-permute-done.3.refs_0_), channel_id=1, source_target_pairs={{0,4},{4,0},{8,12},{12,8},{1,5},{5,1},{9,13},{13,9},{2,6},{6,2},{1... | collective-permute-start | bytes 196616 | tf_op jit(solution)/shard_map/ppermute | solution.py:222
  14.4 4.3 %collective-permute-start.6 = (bf16[1,256,128]{2,1,0:T(8,128)(2,1)S(1)}, bf16[1,256,128]{2,1,0:T(8,128)(2,1)S(1)}, u32[]{:S(2)}, u32[]{:S(2)}) collective-permute-start(bf16[1,256,128]{2,1,0:T(8,128)(2,1)S(1)} %collective-permute-done.5.refs_1_), channel_id=1, source_target_pairs={{0,2},{1,3},{2,0},{3,1},{4,6},{5,7},{6,4},{7,5},{8,10},{9,11},{10,... | collective-permute-start | bytes 196616 | tf_op jit(solution)/shard_map/ppermute | solution.py:222
  15.0 3.9 %collective-permute-start.10 = (bf16[2,256,128]{2,1,0:T(8,128)(2,1)S(1)}, bf16[2,256,128]{2,1,0:T(8,128)(2,1)S(1)}, u32[]{:S(2)}, u32[]{:S(2)}) collective-permute-start(bf16[2,256,128]{2,1,0:T(8,128)(2,1)S(1)} %join.9.refs_2_), channel_id=1, source_target_pairs={{0,1},{1,0},{2,3},{3,2},{4,5},{5,4},{6,7},{7,6},{8,9},{9,8},{10,11... | collective-permute-start | bytes 393224 | tf_op jit(solution)/shard_map/ppermute | solution.py:222
  15.2 3.8 %collective-permute-start.8 = (bf16[2,256,128]{2,1,0:T(8,128)(2,1)S(1)}, bf16[2,256,128]{2,1,0:T(8,128)(2,1)S(1)}, u32[]{:S(2)}, u32[]{:S(2)}) collective-permute-start(bf16[2,256,128]{2,1,0:T(8,128)(2,1)S(1)} %join.7.refs_0_), channel_id=1, source_target_pairs={{0,1},{1,0},{2,3},{3,2},{4,5},{5,4},{6,7},{7,6},{8,9},{9,8},{10,11... | collective-permute-start | bytes 393224 | tf_op jit(solution)/shard_map/ppermute | solution.py:222
  15.8 3.0 %copy-start = (bf16[1,128,512]{2,1,0:T(8,128)(2,1)S(1)}, bf16[1,128,512]{2,1,0:T(8,128)(2,1)}, u32[]{:S(2)}) copy-start(bf16[1,128,512]{2,1,0:T(8,128)(2,1)} %q_ref) | copy-start | bytes 393220
  15.8 3.1 %collective-permute-start.9 = (bf16[2,256,128]{2,1,0:T(8,128)(2,1)S(1)}, bf16[2,256,128]{2,1,0:T(8,128)(2,1)S(1)}, u32[]{:S(2)}, u32[]{:S(2)}) collective-permute-start(bf16[2,256,128]{2,1,0:T(8,128)(2,1)S(1)} %join.8.refs_1_), channel_id=1, source_target_pairs={{0,1},{1,0},{2,3},{3,2},{4,5},{5,4},{6,7},{7,6},{8,9},{9,8},{10,11... | collective-permute-start | bytes 393224 | tf_op jit(solution)/shard_map/ppermute | solution.py:222
  18.8 1.8 %collective-permute-start.7 = (bf16[2,256,128]{2,1,0:T(8,128)(2,1)S(1)}, bf16[2,256,128]{2,1,0:T(8,128)(2,1)S(1)}, u32[]{:S(2)}, u32[]{:S(2)}) collective-permute-start(bf16[2,256,128]{2,1,0:T(8,128)(2,1)S(1)} %join.6.refs_0_), channel_id=1, source_target_pairs={{0,1},{1,0},{2,3},{3,2},{4,5},{5,4},{6,7},{7,6},{8,9},{9,8},{10,11... | collective-permute-start | bytes 393224 | tf_op jit(solution)/shard_map/ppermute | solution.py:222

commit v4 on v1

--- a/solution.py
+++ b/solution.py
@@ -278,7 +278,7 @@
         came = swap(own, "row", flip)
         own = jnp.concatenate([own[0], came[0]]), own[1] + came[1]
         flip //= 2
-    near, far, opposite = (swap(own, "row", flip) for flip in (1, 2, 3))
+    near, far, opposite = (swap(own, "row", flip) for flip in (1, 3, 2))
     own_across = across(own, cols)
     near_across = [swap(piece, "row", 1) for piece in own_across]
     early_places = [place for _, where in (own, *own_across, near, *near_across, far, opposite) for place in where]

time: 19.7 us -> 19.8 us (level)
  waiting for transfers between devices: 4.33 us -> 5.23 us
  starting transfers between devices: 10.9 us -> 10.1 us
    ppermute x11, waiting for transfers between devices: 4.33 us -> 5.23 us  [swap(): lax.ppermute(array, axis, [(i, i ^ flip) for i in range(lax.axis_size(axi...]
    ppermute x11, starting transfers between devices: 10.9 us -> 10.1 us  [swap(): lax.ppermute(array, axis, [(i, i ^ flip) for i in range(lax.axis_size(axi...]
  transfers between devices with their start and end apart: 11 -> 11, of which waited for: 3 -> 4; matrix products, arithmetic and copies ran while one was open for 0% -> 0% of each run, Pallas kernels for 13% -> 13%
where the time goes in v4:
time: 19.8 us; the launch traced here: 19.6 us
  starting transfers between devices  10.1 us (51%)
  waiting for transfers between devices  5.23 us (26%)
  Pallas kernels  3.37 us (17%)
  local copies, waits for them, and re-layouts  0.8 us (4%)
    ppermute x11, starting transfers between devices, swap(): lax.ppermute(array, axis, [(i, i ^ flip) for i in range(lax.axis_size(axi...  10.1 us
    ppermute x11, waiting for transfers between devices, swap(): lax.ppermute(array, axis, [(i, i ^ flip) for i in range(lax.axis_size(axi...  5.23 us
    pallas_call x2, Pallas kernels, attend(): pl.pallas_call(functools.partial(kernel, heads, dense), out_shape=out_sha...  2.27 us
    unnamed x9, local copies, waits for them, and re-layouts  0.79 us
    pallas_call x1, Pallas kernels, per_device(): pl.pallas_call(functools.partial(prepare_kernel, per, places, dense), out...  0.66 us
  transfers between devices with their start and end apart: 11, of which 4 were waited for; matrix products, arithmetic and copies ran while one was open for 0% of the time, Pallas kernels for 13%

profile of v4, /device:TPU:0, one launch (start us, length us, event | category | flops | bytes accessed | tf_op | source)
XLA Modules:
  0.0 19.6 jit_solution(9098809133361617733)
XLA Ops:
  0.0 0.8 %constant_dynamic-update-slice_fusion.1 = bf16[1,256,128]{2,1,0:T(8,128)(2,1)S(1)} fusion(bf16[1,128,128]{2,1,0:T(8,128)(2,1)} %param.6), kind=kLoop, calls=%fused_computation.1 | loop fusion | bytes 65536
  0.8 0.0 copy-done.3
  0.8 3.0 %collective-permute-start.5 = (bf16[1,256,128]{2,1,0:T(8,128)(2,1)S(1)}, bf16[1,256,128]{2,1,0:T(8,128)(2,1)S(1)}, u32[]{:S(2)}, u32[]{:S(2)}) collective-permute-start(bf16[1,256,128]{2,1,0:T(8,128)(2,1)S(1)} %constant_dynamic-update-slice_fusion.refs_0_), channel_id=1, source_target_pairs={{0,2},{1,3},{2,0},{3,1},{4,6},{5,7},{6,4},{7,5},{8,10},{9,11},{10,... | collective-permute-start | bytes 196616 | tf_op jit(solution)/shard_map/ppermute | solution.py:222
  3.8 3.6 %collective-permute-start = (bf16[1,256,128]{2,1,0:T(8,128)(2,1)S(1)}, bf16[1,256,128]{2,1,0:T(8,128)(2,1)S(1)}, u32[]{:S(2)}, u32[]{:S(2)}) collective-permute-start(bf16[1,256,128]{2,1,0:T(8,128)(2,1)S(1)} %constant_dynamic-update-slice_fusion.refs_0_), channel_id=1, source_target_pairs={{0,12},{4,8},{8,4},{12,0},{1,13},{5,9},{9,5},{13,1},{2,14},{6,10},... | collective-permute-start | bytes 196616 | tf_op jit(solution)/shard_map/ppermute | solution.py:222
  7.4 0.0 collective-permute-start.2
  7.4 0.8 %collective-permute-start.6 = (bf16[1,256,128]{2,1,0:T(8,128)(2,1)S(1)}, bf16[1,256,128]{2,1,0:T(8,128)(2,1)S(1)}, u32[]{:S(2)}, u32[]{:S(2)}) collective-permute-start(bf16[1,256,128]{2,1,0:T(8,128)(2,1)S(1)} %constant_dynamic-update-slice_fusion.refs_0_), channel_id=1, source_target_pairs={{0,4},{4,0},{8,12},{12,8},{1,5},{5,1},{9,13},{13,9},{2,6},{6,2},{1... | collective-permute-start | bytes 196616 | tf_op jit(solution)/shard_map/ppermute | solution.py:222
  8.2 0.7 %prepare.1.order_in = s32[1,2,12,512]{3,2,1,0:T(8,128)S(1)} custom-call(s32[4,4,4,4]{3,2,1,0:T(4,128)S(1)} %copy-done.1, s32[4,4,4]{2,1,0:T(4,128)S(1)} %copy-done.2), custom_call_target="tpu_custom_call" | custom-call | tf_op jit(solution)/shard_map/prepare/pallas_call | solution.py:292
  8.9 1.3 %collective-permute-start.7 = (bf16[1,256,128]{2,1,0:T(8,128)(2,1)S(1)}, bf16[1,256,128]{2,1,0:T(8,128)(2,1)S(1)}, u32[]{:S(2)}, u32[]{:S(2)}) collective-permute-start(bf16[1,256,128]{2,1,0:T(8,128)(2,1)S(1)} %collective-permute-done.5.refs_1_), channel_id=1, source_target_pairs={{0,4},{4,0},{8,12},{12,8},{1,5},{5,1},{9,13},{13,9},{2,6},{6,2},{1... | collective-permute-start | bytes 196616 | tf_op jit(solution)/shard_map/ppermute | solution.py:222
  10.2 0.5 %collective-permute-done.refs_0_ = bf16[1,256,128]{2,1,0:T(8,128)(2,1)S(1)} collective-permute-done((bf16[1,256,128]{2,1,0:T(8,128)(2,1)S(1)}, bf16[1,256,128]{2,1,0:T(8,128)(2,1)S(1)}, u32[]{:S(2)}, u32[]{:S(2)}) %collective-permute-start) | collective-permute-done | bytes 65568 | tf_op jit(solution)/shard_map/ppermute | solution.py:222
  10.7 0.1 collective-permute-start.1
  10.7 2.1 %collective-permute-done.2.refs_1_ = bf16[1,256,128]{2,1,0:T(8,128)(2,1)S(1)} collective-permute-done((bf16[1,256,128]{2,1,0:T(8,128)(2,1)S(1)}, bf16[1,256,128]{2,1,0:T(8,128)(2,1)S(1)}, u32[]{:S(2)}, u32[]{:S(2)}) %collective-permute-start.2) | collective-permute-done | bytes 65568 | tf_op jit(solution)/shard_map/ppermute | solution.py:222
  12.8 0.5 %collective-permute-start.3 = (bf16[1,256,128]{2,1,0:T(8,128)(2,1)S(1)}, bf16[1,256,128]{2,1,0:T(8,128)(2,1)S(1)}, u32[]{:S(2)}, u32[]{:S(2)}) collective-permute-start(bf16[1,256,128]{2,1,0:T(8,128)(2,1)S(1)} %collective-permute-done.2.refs_1_), channel_id=1, source_target_pairs={{0,2},{1,3},{2,0},{3,1},{4,6},{5,7},{6,4},{7,5},{8,10},{9,11},{10,... | collective-permute-start | bytes 196616 | tf_op jit(solution)/shard_map/ppermute | solution.py:222
  13.3 0.1 join.9.refs_2_
  13.4 0.1 collective-permute-start.10
  13.5 0.1 join.7.refs_0_
  13.6 0.0 copy-start
  13.6 0.0 collective-permute-done.6.refs_0_
  13.6 0.6 %collective-permute-start.8 = (bf16[2,256,128]{2,1,0:T(8,128)(2,1)S(1)}, bf16[2,256,128]{2,1,0:T(8,128)(2,1)S(1)}, u32[]{:S(2)}, u32[]{:S(2)}) collective-permute-start(bf16[2,256,128]{2,1,0:T(8,128)(2,1)S(1)} %join.7.refs_0_), channel_id=1, source_target_pairs={{0,1},{1,0},{2,3},{3,2},{4,5},{5,4},{6,7},{7,6},{8,9},{9,8},{10,11... | collective-permute-start | bytes 393224 | tf_op jit(solution)/shard_map/ppermute | solution.py:222
  14.1 0.0 collective-permute-done.7.refs_1_
  14.2 0.1 join.8.refs_1_
  14.2 0.1 collective-permute-start.9
  14.3 0.8 %collective-permute-done.1.refs_0_ = bf16[1,256,128]{2,1,0:T(8,128)(2,1)S(1)} collective-permute-done((bf16[1,256,128]{2,1,0:T(8,128)(2,1)S(1)}, bf16[1,256,128]{2,1,0:T(8,128)(2,1)S(1)}, u32[]{:S(2)}, u32[]{:S(2)}) %collective-permute-start.1) | collective-permute-done | bytes 65568 | tf_op jit(solution)/shard_map/ppermute | solution.py:222
  15.1 0.1 turn.1.qt_ref
  15.2 1.9 %collective-permute-done.3.refs_1_ = bf16[1,256,128]{2,1,0:T(8,128)(2,1)S(1)} collective-permute-done((bf16[1,256,128]{2,1,0:T(8,128)(2,1)S(1)}, bf16[1,256,128]{2,1,0:T(8,128)(2,1)S(1)}, u32[]{:S(2)}, u32[]{:S(2)}) %collective-permute-start.3) | collective-permute-done | bytes 65568 | tf_op jit(solution)/shard_map/ppermute | solution.py:222
  17.0 0.1 join.6.refs_0_
  17.1 0.1 collective-permute-start.4
  17.2 0.0 collective-permute-done.10.refs_5_
  17.2 0.0 collective-permute-done.9.refs_4_
  17.2 0.1 join.10.kv_ref
  17.3 1.5 %early.1 = (f32[1,128,512]{2,1,0:T(8,128)S(1)}, f32[1,2,512]{2,1,0:T(2,128)S(1)}) custom-call(bf16[1,128,512]{2,1,0:T(8,128)(2,1)S(1)} %turn.1.qt_ref, s32[1,2,12,512]{3,2,1,0:T(8,128)S(1)} %prepare.1.order_in, bf16[12,256,128]{2,1,0:T(8,128)(2,1)S(1)} %join.10.kv_ref), custom_call_target="tpu_custom_call" | custom-call | tf_op jit(solution)/shard_map/early/pallas_call | solution.py:320
  18.8 0.0 collective-permute-done.4.refs_1_
  18.8 0.8 %last.1 = bf16[1,128,512]{2,1,0:T(8,128)(2,1)} custom-call(bf16[1,128,512]{2,1,0:T(8,128)(2,1)S(1)} %turn.1.qt_ref, s32[1,2,12,512]{3,2,1,0:T(8,128)S(1)} %prepare.1.order_in, bf16[4,256,128]{2,1,0:T(8,128)(2,1)S(1)} %join.11.kv_ref, f32[1,128,512]{2,1,0:T(8,128)S(1)} %get-tuple-element.27.acc_in, f32[1,2,512]{2,1,0:T(2,128)S(1)} %get-tuple-element.28.stats_in), custom_call_target="tpu_custom_call" | custom-call | tf_op jit(solution)/shard_map/last/pallas_call | solution.py:320
  (10 shorter events, 0.0 us)
Async XLA Ops:
  0.0 0.8 %copy-start.3 = (bf16[1,128,128]{2,1,0:T(8,128)(2,1)S(1)}, bf16[1,128,128]{2,1,0:T(8,128)(2,1)}, u32[]{:S(2)}) copy-start(bf16[1,128,128]{2,1,0:T(8,128)(2,1)} %param.7) | copy-start | bytes 98308
  0.8 7.4 %copy-start.1 = (s32[4,4,4,4]{3,2,1,0:T(4,128)S(1)}, s32[4,4,4,4]{3,2,1,0:T(4,128)}, u32[]{:S(2)}) copy-start(s32[4,4,4,4]{3,2,1,0:T(4,128)} %list_hbm.1) | copy-start | bytes 3076
  0.8 7.4 %copy-start.2 = (s32[4,4,4]{2,1,0:T(4,128)S(1)}, s32[4,4,4]{2,1,0:T(4,128)}, u32[]{:S(2)}) copy-start(s32[4,4,4]{2,1,0:T(4,128)} %count_hbm.1) | copy-start | bytes 772
  0.8 8.1 %collective-permute-start.5 = (bf16[1,256,128]{2,1,0:T(8,128)(2,1)S(1)}, bf16[1,256,128]{2,1,0:T(8,128)(2,1)S(1)}, u32[]{:S(2)}, u32[]{:S(2)}) collective-permute-start(bf16[1,256,128]{2,1,0:T(8,128)(2,1)S(1)} %constant_dynamic-update-slice_fusion.refs_0_), channel_id=1, source_target_pairs={{0,2},{1,3},{2,0},{3,1},{4,6},{5,7},{6,4},{7,5},{8,10},{9,11},{10,... | collective-permute-start | bytes 196616 | tf_op jit(solution)/shard_map/ppermute | solution.py:222
  3.8 6.9 %collective-permute-start = (bf16[1,256,128]{2,1,0:T(8,128)(2,1)S(1)}, bf16[1,256,128]{2,1,0:T(8,128)(2,1)S(1)}, u32[]{:S(2)}, u32[]{:S(2)}) collective-permute-start(bf16[1,256,128]{2,1,0:T(8,128)(2,1)S(1)} %constant_dynamic-update-slice_fusion.refs_0_), channel_id=1, source_target_pairs={{0,12},{4,8},{8,4},{12,0},{1,13},{5,9},{9,5},{13,1},{2,14},{6,10},... | collective-permute-start | bytes 196616 | tf_op jit(solution)/shard_map/ppermute | solution.py:222
  7.4 5.4 %collective-permute-start.2 = (bf16[1,256,128]{2,1,0:T(8,128)(2,1)S(1)}, bf16[1,256,128]{2,1,0:T(8,128)(2,1)S(1)}, u32[]{:S(2)}, u32[]{:S(2)}) collective-permute-start(bf16[1,256,128]{2,1,0:T(8,128)(2,1)S(1)} %constant_dynamic-update-slice_fusion.refs_0_), channel_id=1, source_target_pairs={{0,8},{4,12},{8,0},{12,4},{1,9},{5,13},{9,1},{13,5},{2,10},{6,14},... | collective-permute-start | bytes 196616 | tf_op jit(solution)/shard_map/ppermute | solution.py:222
  7.4 6.2 %collective-permute-start.6 = (bf16[1,256,128]{2,1,0:T(8,128)(2,1)S(1)}, bf16[1,256,128]{2,1,0:T(8,128)(2,1)S(1)}, u32[]{:S(2)}, u32[]{:S(2)}) collective-permute-start(bf16[1,256,128]{2,1,0:T(8,128)(2,1)S(1)} %constant_dynamic-update-slice_fusion.refs_0_), channel_id=1, source_target_pairs={{0,4},{4,0},{8,12},{12,8},{1,5},{5,1},{9,13},{13,9},{2,6},{6,2},{1... | collective-permute-start | bytes 196616 | tf_op jit(solution)/shard_map/ppermute | solution.py:222
  8.9 5.3 %collective-permute-start.7 = (bf16[1,256,128]{2,1,0:T(8,128)(2,1)S(1)}, bf16[1,256,128]{2,1,0:T(8,128)(2,1)S(1)}, u32[]{:S(2)}, u32[]{:S(2)}) collective-permute-start(bf16[1,256,128]{2,1,0:T(8,128)(2,1)S(1)} %collective-permute-done.5.refs_1_), channel_id=1, source_target_pairs={{0,4},{4,0},{8,12},{12,8},{1,5},{5,1},{9,13},{13,9},{2,6},{6,2},{1... | collective-permute-start | bytes 196616 | tf_op jit(solution)/shard_map/ppermute | solution.py:222
  10.7 4.4 %collective-permute-start.1 = (bf16[1,256,128]{2,1,0:T(8,128)(2,1)S(1)}, bf16[1,256,128]{2,1,0:T(8,128)(2,1)S(1)}, u32[]{:S(2)}, u32[]{:S(2)}) collective-permute-start(bf16[1,256,128]{2,1,0:T(8,128)(2,1)S(1)} %collective-permute-done.refs_0_), channel_id=1, source_target_pairs={{0,2},{1,3},{2,0},{3,1},{4,6},{5,7},{6,4},{7,5},{8,10},{9,11},{10,... | collective-permute-start | bytes 196616 | tf_op jit(solution)/shard_map/ppermute | solution.py:222
  12.8 4.3 %collective-permute-start.3 = (bf16[1,256,128]{2,1,0:T(8,128)(2,1)S(1)}, bf16[1,256,128]{2,1,0:T(8,128)(2,1)S(1)}, u32[]{:S(2)}, u32[]{:S(2)}) collective-permute-start(bf16[1,256,128]{2,1,0:T(8,128)(2,1)S(1)} %collective-permute-done.2.refs_1_), channel_id=1, source_target_pairs={{0,2},{1,3},{2,0},{3,1},{4,6},{5,7},{6,4},{7,5},{8,10},{9,11},{10,... | collective-permute-start | bytes 196616 | tf_op jit(solution)/shard_map/ppermute | solution.py:222
  13.4 3.8 %collective-permute-start.10 = (bf16[2,256,128]{2,1,0:T(8,128)(2,1)S(1)}, bf16[2,256,128]{2,1,0:T(8,128)(2,1)S(1)}, u32[]{:S(2)}, u32[]{:S(2)}) collective-permute-start(bf16[2,256,128]{2,1,0:T(8,128)(2,1)S(1)} %join.9.refs_2_), channel_id=1, source_target_pairs={{0,1},{1,0},{2,3},{3,2},{4,5},{5,4},{6,7},{7,6},{8,9},{9,8},{10,11... | collective-permute-start | bytes 393224 | tf_op jit(solution)/shard_map/ppermute | solution.py:222
  13.6 1.6 %copy-start = (bf16[1,128,512]{2,1,0:T(8,128)(2,1)S(1)}, bf16[1,128,512]{2,1,0:T(8,128)(2,1)}, u32[]{:S(2)}) copy-start(bf16[1,128,512]{2,1,0:T(8,128)(2,1)} %q_ref) | copy-start | bytes 393220
  13.6 3.6 %collective-permute-start.8 = (bf16[2,256,128]{2,1,0:T(8,128)(2,1)S(1)}, bf16[2,256,128]{2,1,0:T(8,128)(2,1)S(1)}, u32[]{:S(2)}, u32[]{:S(2)}) collective-permute-start(bf16[2,256,128]{2,1,0:T(8,128)(2,1)S(1)} %join.7.refs_0_), channel_id=1, source_target_pairs={{0,1},{1,0},{2,3},{3,2},{4,5},{5,4},{6,7},{7,6},{8,9},{9,8},{10,11... | collective-permute-start | bytes 393224 | tf_op jit(solution)/shard_map/ppermute | solution.py:222
  14.2 3.0 %collective-permute-start.9 = (bf16[2,256,128]{2,1,0:T(8,128)(2,1)S(1)}, bf16[2,256,128]{2,1,0:T(8,128)(2,1)S(1)}, u32[]{:S(2)}, u32[]{:S(2)}) collective-permute-start(bf16[2,256,128]{2,1,0:T(8,128)(2,1)S(1)} %join.8.refs_1_), channel_id=1, source_target_pairs={{0,1},{1,0},{2,3},{3,2},{4,5},{5,4},{6,7},{7,6},{8,9},{9,8},{10,11... | collective-permute-start | bytes 393224 | tf_op jit(solution)/shard_map/ppermute | solution.py:222
  17.1 1.7 %collective-permute-start.4 = (bf16[2,256,128]{2,1,0:T(8,128)(2,1)S(1)}, bf16[2,256,128]{2,1,0:T(8,128)(2,1)S(1)}, u32[]{:S(2)}, u32[]{:S(2)}) collective-permute-start(bf16[2,256,128]{2,1,0:T(8,128)(2,1)S(1)} %join.6.refs_0_), channel_id=1, source_target_pairs={{0,1},{1,0},{2,3},{3,2},{4,5},{5,4},{6,7},{7,6},{8,9},{9,8},{10,11... | collective-permute-start | bytes 393224 | tf_op jit(solution)/shard_map/ppermute | solution.py:222

commit v5 on v2

--- a/solution.py
+++ b/solution.py
@@ -278,7 +278,7 @@
         came = swap(own, "row", flip)
         own = jnp.concatenate([own[0], came[0]]), own[1] + came[1]
         flip //= 2
-    near, far, opposite = (swap(own, "row", flip) for flip in (1, 2, 3))
+    near, far, opposite = (swap(own, "row", flip) for flip in (1, 3, 2))
     own_across = across(own, cols)
     near_across = [swap(piece, "row", 1) for piece in own_across]
     early_places = [place for _, where in (own, *own_across, near, *near_across, far, opposite) for place in where]

time: 20 us -> 19.8 us (0.990)
  starting transfers between devices: 10.8 us -> 10 us
  waiting for transfers between devices: 4.49 us -> 5.27 us
    ppermute x11, starting transfers between devices: 10.8 us -> 10 us  [swap(): lax.ppermute(array, axis, [(i, i ^ flip) for i in range(lax.axis_size(axi...]
    ppermute x11, waiting for transfers between devices: 4.49 us -> 5.27 us  [swap(): lax.ppermute(array, axis, [(i, i ^ flip) for i in range(lax.axis_size(axi...]
  transfers between devices with their start and end apart: 11 -> 11, of which waited for: 2 -> 4; matrix products, arithmetic and copies ran while one was open for 0% -> 0% of each run, Pallas kernels for 13% -> 13%
where the time goes in v5:
time: 19.8 us; the launch traced here: 19.6 us
  starting transfers between devices  10 us (51%)
  waiting for transfers between devices  5.27 us (27%)
  Pallas kernels  3.37 us (17%)
  local copies, waits for them, and re-layouts  0.83 us (4%)
    ppermute x11, starting transfers between devices, swap(): lax.ppermute(array, axis, [(i, i ^ flip) for i in range(lax.axis_size(axi...  10 us
    ppermute x11, waiting for transfers between devices, swap(): lax.ppermute(array, axis, [(i, i ^ flip) for i in range(lax.axis_size(axi...  5.27 us
    pallas_call x2, Pallas kernels, attend(): pl.pallas_call(functools.partial(kernel, heads, dense), out_shape=out_sha...  2.27 us
    unnamed x9, local copies, waits for them, and re-layouts  0.82 us
    pallas_call x1, Pallas kernels, per_device(): pl.pallas_call(functools.partial(prepare_kernel, per, places, dense), out...  0.66 us
  transfers between devices with their start and end apart: 11, of which 4 were waited for; matrix products, arithmetic and copies ran while one was open for 0% of the time, Pallas kernels for 13%

profile of v5, /device:TPU:0, one launch (start us, length us, event | category | flops | bytes accessed | tf_op | source)
XLA Modules:
  0.0 19.6 jit_solution(12444870220212282108)
XLA Ops:
  0.0 0.8 %constant_dynamic-update-slice_fusion.1 = bf16[1,256,128]{2,1,0:T(8,128)(2,1)S(1)} fusion(bf16[1,128,128]{2,1,0:T(8,128)(2,1)} %param.6), kind=kLoop, calls=%fused_computation.1 | loop fusion | bytes 65536
  0.8 0.0 copy-done.3
  0.8 3.0 %collective-permute-start.5 = (bf16[1,256,128]{2,1,0:T(8,128)(2,1)S(1)}, bf16[1,256,128]{2,1,0:T(8,128)(2,1)S(1)}, u32[]{:S(2)}, u32[]{:S(2)}) collective-permute-start(bf16[1,256,128]{2,1,0:T(8,128)(2,1)S(1)} %constant_dynamic-update-slice_fusion.refs_0_), channel_id=1, source_target_pairs={{0,2},{1,3},{2,0},{3,1},{4,6},{5,7},{6,4},{7,5},{8,10},{9,11},{10,... | collective-permute-start | bytes 196616 | tf_op jit(solution)/shard_map/ppermute | solution.py:222
  3.8 3.6 %collective-permute-start = (bf16[1,256,128]{2,1,0:T(8,128)(2,1)S(1)}, bf16[1,256,128]{2,1,0:T(8,128)(2,1)S(1)}, u32[]{:S(2)}, u32[]{:S(2)}) collective-permute-start(bf16[1,256,128]{2,1,0:T(8,128)(2,1)S(1)} %constant_dynamic-update-slice_fusion.refs_0_), channel_id=1, source_target_pairs={{0,12},{4,8},{8,4},{12,0},{1,13},{5,9},{9,5},{13,1},{2,14},{6,10},... | collective-permute-start | bytes 196616 | tf_op jit(solution)/shard_map/ppermute | solution.py:222
  7.4 0.0 collective-permute-start.2
  7.4 0.8 %collective-permute-start.6 = (bf16[1,256,128]{2,1,0:T(8,128)(2,1)S(1)}, bf16[1,256,128]{2,1,0:T(8,128)(2,1)S(1)}, u32[]{:S(2)}, u32[]{:S(2)}) collective-permute-start(bf16[1,256,128]{2,1,0:T(8,128)(2,1)S(1)} %constant_dynamic-update-slice_fusion.refs_0_), channel_id=1, source_target_pairs={{0,4},{4,0},{8,12},{12,8},{1,5},{5,1},{9,13},{13,9},{2,6},{6,2},{1... | collective-permute-start | bytes 196616 | tf_op jit(solution)/shard_map/ppermute | solution.py:222
  8.2 0.0 collective-permute-done.5.refs_1_
  8.2 1.2 %collective-permute-start.7 = (bf16[1,256,128]{2,1,0:T(8,128)(2,1)S(1)}, bf16[1,256,128]{2,1,0:T(8,128)(2,1)S(1)}, u32[]{:S(2)}, u32[]{:S(2)}) collective-permute-start(bf16[1,256,128]{2,1,0:T(8,128)(2,1)S(1)} %collective-permute-done.5.refs_1_), channel_id=1, source_target_pairs={{0,4},{4,0},{8,12},{12,8},{1,5},{5,1},{9,13},{13,9},{2,6},{6,2},{1... | collective-permute-start | bytes 196616 | tf_op jit(solution)/shard_map/ppermute | solution.py:222
  9.4 1.2 %collective-permute-done.refs_0_ = bf16[1,256,128]{2,1,0:T(8,128)(2,1)S(1)} collective-permute-done((bf16[1,256,128]{2,1,0:T(8,128)(2,1)S(1)}, bf16[1,256,128]{2,1,0:T(8,128)(2,1)S(1)}, u32[]{:S(2)}, u32[]{:S(2)}) %collective-permute-start) | collective-permute-done | bytes 65568 | tf_op jit(solution)/shard_map/ppermute | solution.py:222
  10.7 0.0 collective-permute-start.1
  10.7 2.1 %collective-permute-done.2.refs_1_ = bf16[1,256,128]{2,1,0:T(8,128)(2,1)S(1)} collective-permute-done((bf16[1,256,128]{2,1,0:T(8,128)(2,1)S(1)}, bf16[1,256,128]{2,1,0:T(8,128)(2,1)S(1)}, u32[]{:S(2)}, u32[]{:S(2)}) %collective-permute-start.2) | collective-permute-done | bytes 65568 | tf_op jit(solution)/shard_map/ppermute | solution.py:222
  12.8 0.5 %collective-permute-start.3 = (bf16[1,256,128]{2,1,0:T(8,128)(2,1)S(1)}, bf16[1,256,128]{2,1,0:T(8,128)(2,1)S(1)}, u32[]{:S(2)}, u32[]{:S(2)}) collective-permute-start(bf16[1,256,128]{2,1,0:T(8,128)(2,1)S(1)} %collective-permute-done.2.refs_1_), channel_id=1, source_target_pairs={{0,2},{1,3},{2,0},{3,1},{4,6},{5,7},{6,4},{7,5},{8,10},{9,11},{10,... | collective-permute-start | bytes 196616 | tf_op jit(solution)/shard_map/ppermute | solution.py:222
  13.3 0.7 %prepare.1.order_in = s32[1,2,12,512]{3,2,1,0:T(8,128)S(1)} custom-call(s32[4,4,4,4]{3,2,1,0:T(4,128)S(1)} %copy-done.1, s32[4,4,4]{2,1,0:T(4,128)S(1)} %copy-done.2), custom_call_target="tpu_custom_call" | custom-call | tf_op jit(solution)/shard_map/prepare/pallas_call | solution.py:292
  14.0 0.1 join.9.refs_2_
  14.1 0.1 collective-permute-start.10
  14.1 0.1 join.7.refs_0_
  14.2 0.0 copy-start
  14.2 0.0 collective-permute-done.6.refs_0_
  14.2 0.6 %collective-permute-start.8 = (bf16[2,256,128]{2,1,0:T(8,128)(2,1)S(1)}, bf16[2,256,128]{2,1,0:T(8,128)(2,1)S(1)}, u32[]{:S(2)}, u32[]{:S(2)}) collective-permute-start(bf16[2,256,128]{2,1,0:T(8,128)(2,1)S(1)} %join.7.refs_0_), channel_id=1, source_target_pairs={{0,1},{1,0},{2,3},{3,2},{4,5},{5,4},{6,7},{7,6},{8,9},{9,8},{10,11... | collective-permute-start | bytes 393224 | tf_op jit(solution)/shard_map/ppermute | solution.py:222
  14.8 0.0 collective-permute-done.7.refs_1_
  14.8 0.1 join.8.refs_1_
  14.9 0.1 collective-permute-start.9
  15.0 0.1 collective-permute-done.1.refs_0_
  15.1 0.0 copy-done
  15.1 0.1 turn.1.qt_ref
  15.2 1.8 %collective-permute-done.3.refs_1_ = bf16[1,256,128]{2,1,0:T(8,128)(2,1)S(1)} collective-permute-done((bf16[1,256,128]{2,1,0:T(8,128)(2,1)S(1)}, bf16[1,256,128]{2,1,0:T(8,128)(2,1)S(1)}, u32[]{:S(2)}, u32[]{:S(2)}) %collective-permute-start.3) | collective-permute-done | bytes 65568 | tf_op jit(solution)/shard_map/ppermute | solution.py:222
  17.0 0.1 join.6.refs_0_
  17.1 0.1 collective-permute-start.4
  17.2 0.0 collective-permute-done.8.refs_3_
  17.2 0.1 join.10.kv_ref
  17.3 1.5 %early.1 = (f32[1,128,512]{2,1,0:T(8,128)S(1)}, f32[1,2,512]{2,1,0:T(2,128)S(1)}) custom-call(bf16[1,128,512]{2,1,0:T(8,128)(2,1)S(1)} %turn.1.qt_ref, s32[1,2,12,512]{3,2,1,0:T(8,128)S(1)} %prepare.1.order_in, bf16[12,256,128]{2,1,0:T(8,128)(2,1)S(1)} %join.10.kv_ref), custom_call_target="tpu_custom_call" | custom-call | tf_op jit(solution)/shard_map/early/pallas_call | solution.py:319
  18.8 0.8 %last.1 = bf16[1,128,512]{2,1,0:T(8,128)(2,1)} custom-call(bf16[1,128,512]{2,1,0:T(8,128)(2,1)S(1)} %turn.1.qt_ref, s32[1,2,12,512]{3,2,1,0:T(8,128)S(1)} %prepare.1.order_in, bf16[4,256,128]{2,1,0:T(8,128)(2,1)S(1)} %join.11.kv_ref, f32[1,128,512]{2,1,0:T(8,128)S(1)} %get-tuple-element.25.acc_in, f32[1,2,512]{2,1,0:T(2,128)S(1)} %get-tuple-element.26.stats_in), custom_call_target="tpu_custom_call" | custom-call | tf_op jit(solution)/shard_map/last/pallas_call | solution.py:319
  (10 shorter events, 0.0 us)
Async XLA Ops:
  0.0 0.8 %copy-start.3 = (bf16[1,128,128]{2,1,0:T(8,128)(2,1)S(1)}, bf16[1,128,128]{2,1,0:T(8,128)(2,1)}, u32[]{:S(2)}) copy-start(bf16[1,128,128]{2,1,0:T(8,128)(2,1)} %param.7) | copy-start | bytes 98308
  0.8 12.5 %copy-start.1 = (s32[4,4,4,4]{3,2,1,0:T(4,128)S(1)}, s32[4,4,4,4]{3,2,1,0:T(4,128)}, u32[]{:S(2)}) copy-start(s32[4,4,4,4]{3,2,1,0:T(4,128)} %list_hbm.1) | copy-start | bytes 3076
  0.8 12.5 %copy-start.2 = (s32[4,4,4]{2,1,0:T(4,128)S(1)}, s32[4,4,4]{2,1,0:T(4,128)}, u32[]{:S(2)}) copy-start(s32[4,4,4]{2,1,0:T(4,128)} %count_hbm.1) | copy-start | bytes 772
  0.8 7.4 %collective-permute-start.5 = (bf16[1,256,128]{2,1,0:T(8,128)(2,1)S(1)}, bf16[1,256,128]{2,1,0:T(8,128)(2,1)S(1)}, u32[]{:S(2)}, u32[]{:S(2)}) collective-permute-start(bf16[1,256,128]{2,1,0:T(8,128)(2,1)S(1)} %constant_dynamic-update-slice_fusion.refs_0_), channel_id=1, source_target_pairs={{0,2},{1,3},{2,0},{3,1},{4,6},{5,7},{6,4},{7,5},{8,10},{9,11},{10,... | collective-permute-start | bytes 196616 | tf_op jit(solution)/shard_map/ppermute | solution.py:222
  3.8 6.9 %collective-permute-start = (bf16[1,256,128]{2,1,0:T(8,128)(2,1)S(1)}, bf16[1,256,128]{2,1,0:T(8,128)(2,1)S(1)}, u32[]{:S(2)}, u32[]{:S(2)}) collective-permute-start(bf16[1,256,128]{2,1,0:T(8,128)(2,1)S(1)} %constant_dynamic-update-slice_fusion.refs_0_), channel_id=1, source_target_pairs={{0,12},{4,8},{8,4},{12,0},{1,13},{5,9},{9,5},{13,1},{2,14},{6,10},... | collective-permute-start | bytes 196616 | tf_op jit(solution)/shard_map/ppermute | solution.py:222
  7.4 5.4 %collective-permute-start.2 = (bf16[1,256,128]{2,1,0:T(8,128)(2,1)S(1)}, bf16[1,256,128]{2,1,0:T(8,128)(2,1)S(1)}, u32[]{:S(2)}, u32[]{:S(2)}) collective-permute-start(bf16[1,256,128]{2,1,0:T(8,128)(2,1)S(1)} %constant_dynamic-update-slice_fusion.refs_0_), channel_id=1, source_target_pairs={{0,8},{4,12},{8,0},{12,4},{1,9},{5,13},{9,1},{13,5},{2,10},{6,14},... | collective-permute-start | bytes 196616 | tf_op jit(solution)/shard_map/ppermute | solution.py:222
  7.4 6.8 %collective-permute-start.6 = (bf16[1,256,128]{2,1,0:T(8,128)(2,1)S(1)}, bf16[1,256,128]{2,1,0:T(8,128)(2,1)S(1)}, u32[]{:S(2)}, u32[]{:S(2)}) collective-permute-start(bf16[1,256,128]{2,1,0:T(8,128)(2,1)S(1)} %constant_dynamic-update-slice_fusion.refs_0_), channel_id=1, source_target_pairs={{0,4},{4,0},{8,12},{12,8},{1,5},{5,1},{9,13},{13,9},{2,6},{6,2},{1... | collective-permute-start | bytes 196616 | tf_op jit(solution)/shard_map/ppermute | solution.py:222
  8.2 6.6 %collective-permute-start.7 = (bf16[1,256,128]{2,1,0:T(8,128)(2,1)S(1)}, bf16[1,256,128]{2,1,0:T(8,128)(2,1)S(1)}, u32[]{:S(2)}, u32[]{:S(2)}) collective-permute-start(bf16[1,256,128]{2,1,0:T(8,128)(2,1)S(1)} %collective-permute-done.5.refs_1_), channel_id=1, source_target_pairs={{0,4},{4,0},{8,12},{12,8},{1,5},{5,1},{9,13},{13,9},{2,6},{6,2},{1... | collective-permute-start | bytes 196616 | tf_op jit(solution)/shard_map/ppermute | solution.py:222
  10.7 4.4 %collective-permute-start.1 = (bf16[1,256,128]{2,1,0:T(8,128)(2,1)S(1)}, bf16[1,256,128]{2,1,0:T(8,128)(2,1)S(1)}, u32[]{:S(2)}, u32[]{:S(2)}) collective-permute-start(bf16[1,256,128]{2,1,0:T(8,128)(2,1)S(1)} %collective-permute-done.refs_0_), channel_id=1, source_target_pairs={{0,2},{1,3},{2,0},{3,1},{4,6},{5,7},{6,4},{7,5},{8,10},{9,11},{10,... | collective-permute-start | bytes 196616 | tf_op jit(solution)/shard_map/ppermute | solution.py:222
  12.8 4.3 %collective-permute-start.3 = (bf16[1,256,128]{2,1,0:T(8,128)(2,1)S(1)}, bf16[1,256,128]{2,1,0:T(8,128)(2,1)S(1)}, u32[]{:S(2)}, u32[]{:S(2)}) collective-permute-start(bf16[1,256,128]{2,1,0:T(8,128)(2,1)S(1)} %collective-permute-done.2.refs_1_), channel_id=1, source_target_pairs={{0,2},{1,3},{2,0},{3,1},{4,6},{5,7},{6,4},{7,5},{8,10},{9,11},{10,... | collective-permute-start | bytes 196616 | tf_op jit(solution)/shard_map/ppermute | solution.py:222
  14.1 3.1 %collective-permute-start.10 = (bf16[2,256,128]{2,1,0:T(8,128)(2,1)S(1)}, bf16[2,256,128]{2,1,0:T(8,128)(2,1)S(1)}, u32[]{:S(2)}, u32[]{:S(2)}) collective-permute-start(bf16[2,256,128]{2,1,0:T(8,128)(2,1)S(1)} %join.9.refs_2_), channel_id=1, source_target_pairs={{0,1},{1,0},{2,3},{3,2},{4,5},{5,4},{6,7},{7,6},{8,9},{9,8},{10,11... | collective-permute-start | bytes 393224 | tf_op jit(solution)/shard_map/ppermute | solution.py:222
  14.2 0.9 %copy-start = (bf16[1,128,512]{2,1,0:T(8,128)(2,1)S(1)}, bf16[1,128,512]{2,1,0:T(8,128)(2,1)}, u32[]{:S(2)}) copy-start(bf16[1,128,512]{2,1,0:T(8,128)(2,1)} %q_ref) | copy-start | bytes 393220
  14.2 3.0 %collective-permute-start.8 = (bf16[2,256,128]{2,1,0:T(8,128)(2,1)S(1)}, bf16[2,256,128]{2,1,0:T(8,128)(2,1)S(1)}, u32[]{:S(2)}, u32[]{:S(2)}) collective-permute-start(bf16[2,256,128]{2,1,0:T(8,128)(2,1)S(1)} %join.7.refs_0_), channel_id=1, source_target_pairs={{0,1},{1,0},{2,3},{3,2},{4,5},{5,4},{6,7},{7,6},{8,9},{9,8},{10,11... | collective-permute-start | bytes 393224 | tf_op jit(solution)/shard_map/ppermute | solution.py:222
  14.9 2.3 %collective-permute-start.9 = (bf16[2,256,128]{2,1,0:T(8,128)(2,1)S(1)}, bf16[2,256,128]{2,1,0:T(8,128)(2,1)S(1)}, u32[]{:S(2)}, u32[]{:S(2)}) collective-permute-start(bf16[2,256,128]{2,1,0:T(8,128)(2,1)S(1)} %join.8.refs_1_), channel_id=1, source_target_pairs={{0,1},{1,0},{2,3},{3,2},{4,5},{5,4},{6,7},{7,6},{8,9},{9,8},{10,11... | collective-permute-start | bytes 393224 | tf_op jit(solution)/shard_map/ppermute | solution.py:222
  17.1 1.7 %collective-permute-start.4 = (bf16[2,256,128]{2,1,0:T(8,128)(2,1)S(1)}, bf16[2,256,128]{2,1,0:T(8,128)(2,1)S(1)}, u32[]{:S(2)}, u32[]{:S(2)}) collective-permute-start(bf16[2,256,128]{2,1,0:T(8,128)(2,1)S(1)} %join.6.refs_0_), channel_id=1, source_target_pairs={{0,1},{1,0},{2,3},{3,2},{4,5},{5,4},{6,7},{7,6},{8,9},{9,8},{10,11... | collective-permute-start | bytes 393224 | tf_op jit(solution)/shard_map/ppermute | solution.py:222
